TPU v7x, 512 devices: a whole 4x4x16 slice. The times are simulated.
512 devices in a mesh: cell: 64 (over z, y), view: 8 (over x, core).
Axes of the slice: x: 4, y: 4, z: 16, core: 2. Of those that a mesh axis runs over, the one named last changes fastest.
Arguments:
- params: float32 [7, 524288], P(None, 'cell'), may hold values from -4.5 to 4.5
- first_moment: float32 [7, 524288], P(None, 'cell'), may hold values from -6e-05 to 6e-05
- second_moment: float32 [7, 524288], P(None, 'cell'), may hold values from 1e-11 to 1e-08
- camera: float32 [1, 8, 4], P(None, 'view'), may hold values from -0.3 to 0.3
- slot_block: int32 [1, 8, 64, 64, 2], P(None, 'view', 'cell'), may hold values from -1 to 63, as said below
- slot_anchor: float32 [1, 8, 64, 2, 64, 2], P(None, 'view', 'cell'), may hold values from -0.3 to 0.3
- tile_items: int32 [1, 8, 512, 4], P(None, 'view', 'cell'), may hold values from 0 to 127, as said below
- target: float32 [1, 8, 512, 3, 256], P(None, 'view', 'cell'), may hold values from 0 to 1
Outputs:
- new_params: float32 [7, 524288], P(None, 'cell')
- tile_loss: float32 [1, 8, 512], P(None, 'view', 'cell')
Inputs may be any that keep to these rules, and one draw needn't show every extreme that they name: `slot_block`: -1 marks an empty slot; in every step and view each owner receives all 2 slots from some cell. `tile_items`: entry c * 2 + j names the live slot j from cell c to the tile's owner (tile // 8); every live slot is named exactly once, and the 4 entries of a tile come from distinct cells.
All inputs are finite; a program needn't handle non-finite values.
Results may differ from a plain program's by a relative error of at most 0.00035.
Values sent between devices are 32-bit elements; how exact they have to be, the bound alone decides.
A program may use at most 64 MiB of HBM per device.

v0:
```python
import math

import jax
import jax.numpy as jnp
import numpy as np
from jax import lax
from jax.sharding import PartitionSpec as P

SIDE = 16
BLOCK = 128
TAPS = 11


ssim_weight = 0.2
stable_one = 0.0001
stable_two = 0.0009
learn_rate = 0.1
beta_one = 0.9
beta_two = 0.999
adam_eps = 1e-08
first_step = 1
opacity_cap = 0.1
weight_floor = 0.5
highest = lax.Precision.HIGHEST


def sent_together(arrays, axis, split_dim, concat_dim, along):
    columns = [a.reshape(*a.shape[:along], -1) for a in arrays]
    both = jnp.concatenate(columns, axis=along)
    out, at, gathered = (
        lax.all_to_all(both, axis, split_axis=split_dim, concat_axis=concat_dim, tiled=True),
        0,
        [],
    )
    for a, column in zip(arrays, columns):
        share = out[..., at : at + column.shape[along]]
        gathered.append(share.reshape(*share.shape[:along], *a.shape[along:]))
        at += column.shape[along]
    return tuple(gathered)


def split_up(array, dim, count):
    shape = array.shape
    parts = array.reshape(*shape[:dim], count, shape[dim] // count, *shape[dim + 1 :])
    return jnp.moveaxis(parts, dim, 0)


def sum_at_owner(array, axis, dim):
    count = lax.axis_size(axis)
    parts = lax.all_to_all(split_up(array, dim, count), axis, 0, 0, tiled=True)
    return jnp.sum(parts, axis=0)


def laid_out(parts, dim):
    parts = jnp.moveaxis(parts, 0, dim)
    shape = parts.shape
    return parts.reshape(*shape[:dim], shape[dim] * shape[dim + 1], *shape[dim + 2 :])


def copy_for_each(array, axis):
    count = lax.axis_size(axis)
    return lax.all_to_all(
        jnp.broadcast_to(array[None], (count, *array.shape)), axis, 0, 0, tiled=True
    )


def collect(array, axis, dim):
    return laid_out(copy_for_each(array, axis), dim)


def blur_matrix(tile_side, taps_count):
    offsets = np.arange(tile_side)[:, None] - np.arange(tile_side)[None, :]
    kernel = np.exp(-(offsets * offsets) / 4.5) * (np.abs(offsets) <= taps_count // 2)
    kernel = kernel / kernel.sum(axis=1, keepdims=True)
    return jnp.asarray(np.kron(kernel, kernel).T, jnp.float32)


def pixel_grid(tile_side):
    places = jnp.arange(tile_side * tile_side, dtype=jnp.int32)
    grid_x = ((places % tile_side).astype(jnp.float32) + 0.5) / tile_side
    grid_y = ((places // tile_side).astype(jnp.float32) + 0.5) / tile_side
    return (grid_x, grid_y)


def splat_block(block_params, camera_row, anchors, grid_x, grid_y):
    pos_x = block_params[:, 0]
    pos_y = block_params[:, 1]
    mean_u = (1.0 + camera_row[0]) * pos_x + camera_row[1] * pos_y + anchors[:, 0:1]
    mean_w = camera_row[2] * pos_x + (1.0 + camera_row[3]) * pos_y + anchors[:, 1:2]
    inverse = 0.5 * jnp.exp(-2.0 * block_params[:, 2])
    opacity = opacity_cap * jax.nn.sigmoid(block_params[:, 3])
    colours = jax.nn.sigmoid(block_params[:, 4:7])
    delta_x = grid_x[None, None, :] - mean_u[:, :, None]
    delta_y = grid_y[None, None, :] - mean_w[:, :, None]
    alphas = opacity[:, :, None] * jnp.exp(
        -(delta_x * delta_x + delta_y * delta_y) * inverse[:, :, None]
    )
    weighted = jnp.einsum("ncg,ngp->ncp", colours, alphas, precision=highest)
    totals = jnp.sum(alphas, axis=1)
    transmit = jnp.exp(jnp.sum(jnp.log1p(-alphas), axis=1))
    shaded = (1.0 - transmit)[:, None, :] * weighted / jnp.maximum(totals, weight_floor)[:, None, :]
    return jnp.concatenate([shaded, transmit[:, None, :]], axis=1)


def merge_tiles(items):
    fronts = jnp.ones_like(items[:, 0, 3])
    images = jnp.zeros_like(items[:, 0, :3])
    for rank_index in range(items.shape[1]):
        images = images + fronts[:, None, :] * items[:, rank_index, :3]
        fronts = fronts * items[:, rank_index, 3]
    return images


def tile_losses(images, goal_tiles, blur_table):
    tile_count = images.shape[0]
    predicted = images.reshape(tile_count * 3, -1)
    wanted = goal_tiles.reshape(tile_count * 3, -1)
    stacked = jnp.concatenate(
        [predicted, wanted, predicted * predicted, wanted * wanted, predicted * wanted], axis=0
    )
    blurred = jnp.dot(stacked, blur_table, precision=highest, preferred_element_type=jnp.float32)
    local_pred, local_goal, square_pred, square_goal, cross_term = jnp.split(blurred, 5, axis=0)
    var_pred = square_pred - local_pred * local_pred
    var_goal = square_goal - local_goal * local_goal
    cov_both = cross_term - local_pred * local_goal
    similar = (
        (2.0 * local_pred * local_goal + stable_one)
        * (2.0 * cov_both + stable_two)
        / (
            (local_pred * local_pred + local_goal * local_goal + stable_one)
            * (var_pred + var_goal + stable_two)
        )
    )
    residue = predicted - wanted
    values = (1.0 - ssim_weight) * residue * residue + ssim_weight * (1.0 - similar)
    return jnp.mean(values.reshape(tile_count, -1), axis=1)


def in_groups(function, operands, groups):
    shaped = jax.tree.map(
        lambda array: array.reshape((groups, array.shape[0] // groups) + array.shape[1:]), operands
    )
    results = lax.map(lambda pieces: function(*pieces), shaped)
    return jax.tree.map(lambda array: array.reshape((-1,) + array.shape[2:]), results)


def shards(
    params, first_moment, second_moment, camera, slot_block, slot_anchor, tile_items, target
):
    cell_count = lax.axis_size("cell")
    capacity = slot_block.shape[-1]
    tile_dev = tile_items.shape[2]
    depth_count = tile_items.shape[3]
    components = params.shape[0]
    per_cell = params.shape[1]
    block_count = per_cell // BLOCK
    pixels = SIDE * SIDE
    blur_table = blur_matrix(SIDE, TAPS)
    grid_x, grid_y = pixel_grid(SIDE)
    slot_total = cell_count * capacity
    tile_groups = math.gcd(tile_dev, 8)
    current = params
    share_size = per_cell // lax.axis_size("view")
    offset = lax.axis_index("view") * share_size
    moment_one = lax.dynamic_slice_in_dim(first_moment, offset, share_size, 1)
    moment_two = lax.dynamic_slice_in_dim(second_moment, offset, share_size, 1)
    camera_row = camera[0, 0]
    block_ids = slot_block[0, 0, 0].reshape(-1)
    is_live = block_ids >= 0
    safe_ids = jnp.maximum(block_ids, 0)
    anchors = slot_anchor[0, 0, 0].reshape(2, -1).T
    blocks = jnp.transpose(
        jnp.take(current.reshape(components, block_count, BLOCK), safe_ids, axis=1), (1, 0, 2)
    )
    entries = tile_items[0, 0].reshape(-1)
    goal_tiles = target[0, 0]
    arrived, arrived_anchors = sent_together(
        (
            blocks.reshape(cell_count, capacity, components, BLOCK),
            anchors.reshape(cell_count, capacity, 2),
        ),
        "cell",
        0,
        0,
        2,
    )
    item_params = jnp.take(arrived.reshape(slot_total, components, BLOCK), entries, axis=0)
    item_anchors = jnp.take(arrived_anchors.reshape(slot_total, 2), entries, axis=0)

    def owner_group(group_params, group_anchors, group_goals):

        def group_loss(inner_params):
            partial_value = splat_block(inner_params, camera_row, group_anchors, grid_x, grid_y)
            return tile_losses(
                merge_tiles(partial_value.reshape(-1, depth_count, 4, pixels)),
                group_goals,
                blur_table,
            )

        group_values, back_fn = jax.vjp(group_loss, group_params)
        return (group_values, back_fn(jnp.ones_like(group_values))[0])

    losses, item_grads = in_groups(
        owner_group, (item_params, item_anchors, goal_tiles), tile_groups
    )
    returned = jnp.zeros((slot_total, components, BLOCK), jnp.float32).at[entries].set(item_grads)
    slot_grads = lax.all_to_all(
        returned.reshape(cell_count, capacity, components, BLOCK),
        "cell",
        split_axis=0,
        concat_axis=0,
        tiled=True,
    ).reshape(slot_total, components, BLOCK)
    loss_rows = [losses]
    selector = ((safe_ids[:, None] == jnp.arange(block_count)[None, :]) & is_live[:, None]).astype(
        jnp.float32
    )
    gradient = jnp.einsum("nb,nck->cbk", selector, slot_grads, precision=highest).reshape(
        components, per_cell
    )
    fix_one = 1.0 - beta_one**first_step
    fix_two = 1.0 - beta_two**first_step
    piece_grad = sum_at_owner(gradient, "view", 1)
    moment_one = beta_one * moment_one + (1.0 - beta_one) * piece_grad
    moment_two = beta_two * moment_two + (1.0 - beta_two) * piece_grad * piece_grad
    owned_part = lax.dynamic_slice_in_dim(current, offset, share_size, 1)
    owned_part = owned_part - learn_rate * (moment_one / fix_one) / (
        jnp.sqrt(moment_two / fix_two) + adam_eps
    )
    current = collect(owned_part, "view", 1)
    return (current, jnp.stack(loss_rows)[:, None, :])


def solution(mesh):
    placed = (
        P(None, "cell"),
        P(None, "cell"),
        P(None, "cell"),
        P(None, "view", None),
        P(None, "view", "cell", None, None),
        P(None, "view", "cell", None, None, None),
        P(None, "view", "cell", None),
        P(None, "view", "cell", None, None),
    )
    return jax.shard_map(
        shards,
        mesh=mesh,
        in_specs=placed,
        out_specs=(P(None, "cell"), P(None, "view", "cell")),
        check_vma=False,
    )
```

profile of v0, /device:TPU:1, one launch (start us, length us, event | category | flops | bytes accessed | tf_op | source)
XLA Modules:
  0.0 197.0 jit_solution(4218209914570203675)
XLA Ops:
  4.9 19.4 %all-to-all-start = ((f32[64,2,898]{2,1,0:T(2,128)}), f32[64,2,898]{2,1,0:T(2,128)S(1)}, u32[]{:S(2)}, u32[]{:S(2)}) async-start(f32[64,2,898]{2,1,0:T(2,128)} %pad_maximum_fusion), calls=%async_computation | async-start | bytes 1048576 | tf_op jit(solution)/shard_map/all_to_all | solution.py:31
  27.7 26.6 %all-to-all-done = f32[64,2,898]{2,1,0:T(2,128)S(1)} async-done(((f32[64,2,898]{2,1,0:T(2,128)}), f32[64,2,898]{2,1,0:T(2,128)S(1)}, u32[]{:S(2)}, u32[]{:S(2)}) %all-to-all-start) | async-done | bytes 459808 | tf_op jit(solution)/shard_map/all_to_all | solution.py:31
  56.5 74.6 %while.17 = (s32[]{:T(128)}, f32[8,1]{0,1:T(1,128)S(1)}, f32[8,4,7,128]{3,2,1,0:T(8,128)S(1)}, f32[8,4,7,128]{3,2,1,0:T(8,128)S(1)}, f32[]{:T(128)}, /*index=5*/...) while((s32[]{:T(128)}, f32[8,1]{0,1:T(1,128)S(1)}, ...), condition=%wide.region_13.14_spmd.clone.clone, body=%wide.region_0.13_spmd.sunk.clone.clone.sunk | while | flops 45164544 | bytes 1323393 | solution.py:143
  57.2 1.3 broadcast_multiply_fusion.7
  62.2 1.4 fusion.136
  64.4 1.3 multiply_add_fusion.11
  66.5 1.3 broadcast_multiply_fusion.7
  71.5 1.4 fusion.136
  73.8 1.3 multiply_add_fusion.11
  75.8 1.3 broadcast_multiply_fusion.7
  80.9 1.4 fusion.136
  83.1 1.3 multiply_add_fusion.11
  85.2 1.3 broadcast_multiply_fusion.7
  90.2 1.4 fusion.136
  92.4 1.3 multiply_add_fusion.11
  94.5 1.3 broadcast_multiply_fusion.7
  99.6 1.4 fusion.136
  101.8 1.3 multiply_add_fusion.11
  103.8 1.3 broadcast_multiply_fusion.7
  108.9 1.4 fusion.136
  111.1 1.3 multiply_add_fusion.11
  113.2 1.3 broadcast_multiply_fusion.7
  118.2 1.4 fusion.136
  120.5 1.3 multiply_add_fusion.11
  122.5 1.3 broadcast_multiply_fusion.7
  127.6 1.4 fusion.136
  131.7 1.5 scatter_fusion
  134.2 8.0 %all-to-all-start.1 = ((f32[64,2,7,128]{3,1,2,0:T(2,128)}), f32[64,2,7,128]{3,1,2,0:T(2,128)S(1)}, u32[]{:S(2)}, u32[]{:S(2)}) async-start(f32[64,2,7,128]{3,1,2,0:T(2,128)} %copy.46), calls=%async_computation.1 | async-start | bytes 917504 | tf_op jit(solution)/shard_map/all_to_all | solution.py:207
  142.5 26.2 %all-to-all-done.1 = f32[64,2,7,128]{3,1,2,0:T(2,128)S(1)} async-done(((f32[64,2,7,128]{3,1,2,0:T(2,128)}), f32[64,2,7,128]{3,1,2,0:T(2,128)S(1)}, u32[]{:S(2)}, u32[]{:S(2)}) %all-to-all-start.1) | async-done | bytes 458784 | tf_op jit(solution)/shard_map/all_to_all | solution.py:207
  170.1 8.8 %all-to-all-start.2 = ((f32[8,7,1024]{2,1,0:T(8,128)}), f32[8,7,1024]{2,1,0:T(8,128)S(1)}, u32[]{:S(2)}, u32[]{:S(2)}) async-start(f32[8,7,1024]{2,1,0:T(8,128)} %bitcast.126), calls=%async_computation.2 | async-start | bytes 524288 | tf_op jit(solution)/shard_map/all_to_all | solution.py:50
  178.9 6.5 %all-to-all-done.2 = f32[8,7,1024]{2,1,0:T(8,128)S(1)} async-done(((f32[8,7,1024]{2,1,0:T(8,128)}), f32[8,7,1024]{2,1,0:T(8,128)S(1)}, u32[]{:S(2)}, u32[]{:S(2)}) %all-to-all-start.2) | async-done | bytes 229408 | tf_op jit(solution)/shard_map/all_to_all | solution.py:50
  186.3 9.9 %all_to_all.20 = f32[8,7,1024]{2,1,0:T(8,128)S(1)} all-to-all(f32[8,7,1024]{2,1,0:T(8,128)S(1)} %broadcast_in_dim.130), channel_id=1, replica_groups=mesh['cell'=64,'view'=8] {'view'}, dimensions={0} | all-to-all | bytes 458752 | tf_op jit(solution)/shard_map/all_to_all | solution.py:62
  (370 shorter events, 50.6 us)
Async XLA Ops:
  0.6 2.0 %copy-start.1 = (f32[7,8192]{1,0:T(8,128)S(1)}, f32[7,8192]{1,0:T(8,128)}, u32[]{:S(2)}) copy-start(f32[7,8192]{1,0:T(8,128)} %param.11) | copy-start | bytes 688132
  4.9 22.7 %copy-start.3 = (f32[1,1,8,3,256]{4,2,3,1,0:T(8,128)S(1)}, f32[1,1,8,3,256]{4,2,3,1,0:T(8,128)}, u32[]{:S(2)}) copy-start(f32[1,1,8,3,256]{4,2,3,1,0:T(8,128)} %param.18) | copy-start | bytes 73732
  4.9 49.4 %all-to-all-start = ((f32[64,2,898]{2,1,0:T(2,128)}), f32[64,2,898]{2,1,0:T(2,128)S(1)}, u32[]{:S(2)}, u32[]{:S(2)}) async-start(f32[64,2,898]{2,1,0:T(2,128)} %pad_maximum_fusion), calls=%async_computation | async-start | bytes 1048576 | tf_op jit(solution)/shard_map/all_to_all | solution.py:31
  24.4 0.7 copy-start.4
  25.1 0.7 copy-start.2
  55.6 1.0 copy-start
  131.2 0.5 copy-start.6
  134.2 8.0 %copy-start.5 = (s32[1,1,1,64,2]{3,4,2,1,0:T(2,128)S(1)}, s32[1,1,1,64,2]{3,4,2,1,0:T(2,128)}, u32[]{:S(2)}) copy-start(s32[1,1,1,64,2]{3,4,2,1,0:T(2,128)} %param.15) | copy-start | bytes 1540
  134.2 34.5 %all-to-all-start.1 = ((f32[64,2,7,128]{3,1,2,0:T(2,128)}), f32[64,2,7,128]{3,1,2,0:T(2,128)S(1)}, u32[]{:S(2)}, u32[]{:S(2)}) async-start(f32[64,2,7,128]{3,1,2,0:T(2,128)} %copy.46), calls=%async_computation.1 | async-start | bytes 917504 | tf_op jit(solution)/shard_map/all_to_all | solution.py:207
  170.1 15.3 %all-to-all-start.2 = ((f32[8,7,1024]{2,1,0:T(8,128)}), f32[8,7,1024]{2,1,0:T(8,128)S(1)}, u32[]{:S(2)}, u32[]{:S(2)}) async-start(f32[8,7,1024]{2,1,0:T(8,128)} %bitcast.126), calls=%async_computation.2 | async-start | bytes 524288 | tf_op jit(solution)/shard_map/all_to_all | solution.py:50
where the time goes:
time: 198 us; the launch traced here: 197 us
  waiting for transfers between devices  59.4 us (30%)
  starting transfers between devices  36.3 us (18%)
  other arithmetic  35.6 us (18%)
  matrix products  26.9 us (14%)
  local copies, waits for them, and re-layouts  19.9 us (10%)
  blocking collectives  9.95 us (5%)
  loops' own time  6.84 us (3%)
  between operations  2.11 us (1%)
    all_to_all x1, waiting for transfers between devices, sent_together(): lax.all_to_all(both, axis, split_axis=split_dim, concat_axis=concat_dim,...  26.6 us
    all_to_all x1, waiting for transfers between devices, shards(): lax.all_to_all(returned.reshape(cell_count, capacity, components, BLOCK),...  26.2 us
    dot_general x24, matrix products, splat_block(): weighted = jnp.einsum('ncg,ngp->ncp', colours, alphas, precision=highest)  22.9 us
    all_to_all x1, starting transfers between devices, sent_together(): lax.all_to_all(both, axis, split_axis=split_dim, concat_axis=concat_dim,...  19.4 us
    mul x24, other arithmetic, splat_block(): opacity = opacity_cap * jax.nn.sigmoid(block_params[:, 3])  10.3 us
    add_any x8, other arithmetic, splat_block(): (1.0 + camera_row[0]) * pos_x + camera_row[1] * pos_y + anchors[:, 0:1]  10.1 us
    all_to_all x1, blocking collectives, copy_for_each(): lax.all_to_all(jnp.broadcast_to(array[None], (count, *array.shape)), axis...  9.95 us
    all_to_all x1, starting transfers between devices, sum_at_owner(): parts = lax.all_to_all(split_up(array, dim, count), axis, 0, 0, tiled=True)  8.84 us
  transfers between devices with their start and end apart: 3, of which 3 were waited for; matrix products, arithmetic and copies ran while one was open for 1% of the time, Pallas kernels for 0%

commit v1 on v0

v1 whole, which is shorter than its diff:
```python
import functools

import jax
import jax.numpy as jnp
import numpy as np
from jax import lax
from jax.experimental import pallas as pl
from jax.experimental.pallas import tpu as pltpu
from jax.sharding import PartitionSpec as P

SIDE = 16
PIX = 256
BLOCK = 128
COMP = 7
TAPS = 11
DEPTH = 4
TILES = 8
NCELL = 64
NVIEW = 8
NBLOCK = 64
CAP = 2
NZ = 16
NY = 4
GROUP = 8

SSIM_WEIGHT = 0.2
STABLE_ONE = 0.0001
STABLE_TWO = 0.0009
LEARN_RATE = 0.1
BETA_ONE = 0.9
BETA_TWO = 0.999
ADAM_EPS = 1e-08
FIRST_STEP = 1
OPACITY_CAP = 0.1
WEIGHT_FLOOR = 0.5

F32 = jnp.float32
MESH = pl.DeviceIdType.MESH
HIGHEST = lax.Precision.HIGHEST


def blur_matrix():
    offsets = np.arange(SIDE)[:, None] - np.arange(SIDE)[None, :]
    kernel = np.exp(-(offsets * offsets) / 4.5) * (np.abs(offsets) <= TAPS // 2)
    kernel = kernel / kernel.sum(axis=1, keepdims=True)
    return jnp.asarray(np.kron(kernel, kernel).T, F32)


def cell_peer(i, z, y):
    k = lax.div(i, NY)
    m = lax.div(k + 1, 2)
    dz = jnp.where(lax.rem(k, 2) == 1, m, NZ - m)
    return lax.rem(z + dz, NZ) * NY + lax.rem(y + i, NY)


def send_blocks(camera_ref, ids_ref, anchor_ref, params_ref, out_ref, derived, tx, send_sem, recv_sem):
    c = lax.axis_index("cell")
    v = lax.axis_index("view")
    z, y = lax.div(c, NY), lax.rem(c, NY)
    barrier = pltpu.get_barrier_semaphore()

    @pl.loop(1, NCELL, unroll=9)
    def _(i):
        pl.semaphore_signal(
            barrier, inc=1, device_id=(cell_peer(i, z, y), v), device_id_type=MESH
        )

    q0, q1, q2, q3 = (camera_ref[0, i] for i in range(4))
    width = 1024
    for part in range(NBLOCK * BLOCK // width):
        lanes = pl.ds(part * width, width)
        values = params_ref[:, lanes]
        row = lax.broadcasted_iota(jnp.int32, values.shape, 0)
        logistic = 1.0 / (1.0 + jnp.exp(-values))
        inverse = 0.5 * jnp.exp(-2.0 * values)
        pos_x, pos_y = values[0:1], values[1:2]
        base_u = (1.0 + q0) * pos_x + q1 * pos_y
        base_w = q2 * pos_x + (1.0 + q3) * pos_y
        out = jnp.where(row == 3, OPACITY_CAP * logistic, logistic)
        out = jnp.where(row == 2, inverse, out)
        out = jnp.where(row == 1, base_w, out)
        out = jnp.where(row == 0, base_u, out)
        for i in range(width // BLOCK):
            derived[1 + part * (width // BLOCK) + i] = out[:, i * BLOCK : (i + 1) * BLOCK]
    derived[0] = jnp.zeros((COMP, BLOCK), F32)

    pl.semaphore_wait(barrier, NCELL - 1)

    def gather(o):
        row = lax.broadcasted_iota(jnp.int32, (COMP, BLOCK), 0)
        for j in range(CAP):
            tile = derived[ids_ref[j, o] + 1]
            shift = jnp.where(
                row == 0, anchor_ref[j, o], jnp.where(row == 1, anchor_ref[CAP + j, o], 0.0)
            )
            tx[o, j] = tile + shift

    @pl.loop(1, NCELL, unroll=3)
    def _(i):
        o = cell_peer(i, z, y)
        gather(o)
        pltpu.make_async_remote_copy(
            src_ref=tx.at[o],
            dst_ref=out_ref.at[c],
            send_sem=send_sem,
            recv_sem=recv_sem,
            device_id=(o, v),
            device_id_type=MESH,
        ).start()

    gather(c)
    pltpu.make_async_copy(tx.at[c], out_ref.at[c], recv_sem).start()
    pltpu.make_async_copy(tx, out_ref, recv_sem).wait()
    rest = pl.ds(0, NCELL - 1)
    pltpu.make_async_copy(tx.at[rest], out_ref.at[rest], send_sem).wait()


def render(camera_ref, items_ref, rx_ref, goal_ref, blur_ref, grad_ref, loss_ref, alphas, merged, back):
    lane = lax.broadcasted_iota(jnp.int32, (GROUP, 128), 1)
    level = lax.broadcasted_iota(jnp.int32, (GROUP, 128), 0)
    grid_x = ((lane & (SIDE - 1)).astype(F32) + 0.5) / SIDE
    grid_y = [((lane >> 4).astype(F32) + (0.5 + half * 8)) / SIDE for half in range(2)]
    halves = [pl.ds(0, 128), pl.ds(128, 128)]

    def columns(e):
        tile = rx_ref[e >> 1, e & 1]
        return tile, jnp.transpose(jnp.concatenate([tile, jnp.zeros((1, BLOCK), F32)], axis=0))

    def spread(cols, g, i):
        return jnp.broadcast_to(cols[g * GROUP : (g + 1) * GROUP, i : i + 1], (GROUP, 128))

    @pl.loop(0, TILES)
    def _(t):
        for k in range(DEPTH):
            _, cols = columns(items_ref[k, t])
            slot = t * DEPTH + k
            clear = [jnp.ones((GROUP, 128), F32) for _ in range(2)]
            sums = [[jnp.zeros((GROUP, 128), F32) for _ in range(4)] for _ in range(2)]
            for g in range(BLOCK // GROUP):
                u, w, inverse, opacity, c0, c1, c2 = (spread(cols, g, i) for i in range(COMP))
                dx = grid_x - u
                dx2 = dx * dx
                for half in range(2):
                    dy = grid_y[half] - w
                    alpha = opacity * jnp.exp(-(dx2 + dy * dy) * inverse)
                    alphas[slot, pl.ds(g * GROUP, GROUP), halves[half]] = alpha
                    clear[half] = clear[half] * (1.0 - alpha)
                    s = sums[half]
                    s[0] = s[0] + alpha
                    s[1] = s[1] + c0 * alpha
                    s[2] = s[2] + c1 * alpha
                    s[3] = s[3] + c2 * alpha
            for half in range(2):
                p = clear[half]
                for step in (4, 2, 1):
                    p = p * pltpu.roll(p, step, 0)
                for i, whole in enumerate([p, *sums[half]]):
                    if i:
                        whole = jnp.sum(whole, axis=0, keepdims=True)
                    merged[i, k, :, halves[half]] = jnp.where(
                        level == t, whole, merged[i, k, :, halves[half]]
                    )

    fronts = [jnp.ones((TILES, PIX), F32)]
    images = [jnp.zeros((TILES, PIX), F32) for _ in range(3)]
    colours = []
    for k in range(DEPTH):
        transmit, total = merged[0, k], merged[1, k]
        scale = (1.0 - transmit) / jnp.maximum(total, WEIGHT_FLOOR)
        shaded = [scale * merged[2 + ch, k] for ch in range(3)]
        images = [images[ch] + fronts[k] * shaded[ch] for ch in range(3)]
        colours.append(shaded)
        fronts.append(fronts[k] * transmit)

    a = jnp.concatenate(images, axis=0)
    b = jnp.concatenate([goal_ref[ch] for ch in range(3)], axis=0)
    rows = 3 * TILES
    blurred = jnp.dot(
        jnp.concatenate([a, b, a * a, b * b, a * b], axis=0),
        blur_ref[...],
        precision=HIGHEST,
        preferred_element_type=F32,
    )
    ma, mb, saa, sbb, sab = (blurred[i * rows : (i + 1) * rows] for i in range(5))
    va = saa - ma * ma
    vb = sbb - mb * mb
    cab = sab - ma * mb
    n1 = 2.0 * ma * mb + STABLE_ONE
    n2 = 2.0 * cab + STABLE_TWO
    d1 = ma * ma + mb * mb + STABLE_ONE
    d2 = va + vb + STABLE_TWO
    under = 1.0 / (d1 * d2)
    ssim = n1 * n2 * under
    apart = a - b
    values = (1.0 - SSIM_WEIGHT) * apart * apart + SSIM_WEIGHT * (1.0 - ssim)
    per_tile = values[0:TILES] + values[TILES : 2 * TILES] + values[2 * TILES :]
    count = 3.0 * PIX
    loss = jnp.sum(per_tile, axis=1, keepdims=True) / count
    sub = lax.broadcasted_iota(jnp.int32, (TILES, TILES), 0)
    col = lax.broadcasted_iota(jnp.int32, (TILES, TILES), 1)
    loss_ref[...] = jnp.sum(jnp.where(sub == col, loss, 0.0), axis=0, keepdims=True)

    g_s = -SSIM_WEIGHT / count
    g_n1 = g_s * n2 * under
    g_n2 = g_s * n1 * under
    g_d1 = -g_s * ssim / d1
    g_d2 = -g_s * ssim / d2
    g_ab = 2.0 * g_n2
    g_ma = 2.0 * mb * g_n1 + 2.0 * ma * g_d1 - mb * g_ab - 2.0 * ma * g_d2
    backed = lax.dot_general(
        jnp.concatenate([g_ma, g_d2, g_ab], axis=0),
        blur_ref[...],
        (((1,), (1,)), ((), ())),
        precision=HIGHEST,
        preferred_element_type=F32,
    )
    g_image = (
        (2.0 * (1.0 - SSIM_WEIGHT) / count) * apart
        + backed[0:rows]
        + 2.0 * a * backed[rows : 2 * rows]
        + b * backed[2 * rows :]
    )
    g_ch = [g_image[ch * TILES : (ch + 1) * TILES] for ch in range(3)]
    g_front = jnp.zeros((TILES, PIX), F32)
    for k in reversed(range(DEPTH)):
        transmit, total = merged[0, k], merged[1, k]
        floor = jnp.maximum(total, WEIGHT_FLOOR)
        over = 1.0 / floor
        shade = (1.0 - transmit) * over
        lit = sum(g_ch[ch] * merged[2 + ch, k] for ch in range(3)) * over * fronts[k]
        g_transmit = fronts[k] * g_front - lit
        share = jnp.where(total > WEIGHT_FLOOR, 1.0, jnp.where(total == WEIGHT_FLOOR, 0.5, 0.0))
        ways = [fronts[k] * g_ch[ch] * shade for ch in range(3)]
        for i, way in enumerate([*ways, -share * lit * shade, g_transmit * transmit]):
            for half in range(2):
                back[i, k, half] = way[:, half * 128 : (half + 1) * 128]
        g_front = sum(g_ch[ch] * colours[k][ch] for ch in range(3)) + transmit * g_front

    @pl.loop(0, NCELL)
    def _(i):
        grad_ref[i] = jnp.zeros((CAP, COMP, BLOCK), F32)

    q0, q1, q2, q3 = (camera_ref[0, i] for i in range(4))

    @pl.loop(0, TILES)
    def _(t):
        for k in range(DEPTH):
            e = items_ref[k, t]
            tile, cols = columns(e)
            slot = t * DEPTH + k
            rays = [
                [
                    jnp.broadcast_to(back[i, k, half, pl.ds(t, 1), :], (GROUP, 128))
                    for half in range(2)
                ]
                for i in range(5)
            ]
            pieces = []
            for g in range(BLOCK // GROUP):
                u, w, _, _, c0, c1, c2 = (spread(cols, g, i) for i in range(COMP))
                dx = grid_x - u
                q_sum = qy = qr = None
                tints = [None] * 3
                for half in range(2):
                    alpha = alphas[slot, pl.ds(g * GROUP, GROUP), halves[half]]
                    dy = grid_y[half] - w
                    slope = (
                        c0 * rays[0][half]
                        + c1 * rays[1][half]
                        + c2 * rays[2][half]
                        + rays[3][half]
                        - rays[4][half] / (1.0 - alpha)
                    )
                    q = slope * alpha
                    qd = q * dy
                    parts = [q, qd, qd * dy] + [rays[ch][half] * alpha for ch in range(3)]
                    if half == 0:
                        q_sum, qy, qr, *tints = parts
                    else:
                        q_sum, qy, qr = q_sum + parts[0], qy + parts[1], qr + parts[2]
                        tints = [tints[ch] + parts[3 + ch] for ch in range(3)]
                qx = q_sum * dx
                qr = qr + qx * dx
                lane8 = lax.broadcasted_iota(jnp.int32, (GROUP, GROUP), 1)
                piece = jnp.zeros((GROUP, GROUP), F32)
                for i, value in enumerate([qx, qy, qr, q_sum, *tints]):
                    piece = jnp.where(lane8 == i, jnp.sum(value, axis=1, keepdims=True), piece)
                pieces.append(piece)
            sums = jnp.transpose(jnp.concatenate(pieces, axis=0))
            twice = 2.0 * tile[2:3]
            du = twice * sums[0:1]
            dw = twice * sums[1:2]
            tone = tile[4:7]
            grad_ref[e >> 1, e & 1] = jnp.concatenate(
                [
                    (1.0 + q0) * du + q2 * dw,
                    q1 * du + (1.0 + q3) * dw,
                    twice * sums[2:3],
                    (1.0 - tile[3:4] / OPACITY_CAP) * sums[3:4],
                    tone * (1.0 - tone) * sums[4:7],
                ],
                axis=0,
            )


def return_and_step(
    grad_ref, ids_ref, params_ref, first_ref, second_ref, out_ref,
    rx, spread, shares, rows, mine, send_sem, recv_sem, part_send, part_recv, row_send, row_recv,
):
    c = lax.axis_index("cell")
    v = lax.axis_index("view")
    z, y = lax.div(c, NY), lax.rem(c, NY)
    barrier = pltpu.get_barrier_semaphore()

    @pl.loop(1, NCELL, unroll=9)
    def _(i):
        pl.semaphore_signal(
            barrier, inc=1, device_id=(cell_peer(i, z, y), v), device_id_type=MESH
        )

    for i in range(1, NVIEW):
        pl.semaphore_signal(
            barrier, inc=1, device_id=(c, lax.rem(v + i, NVIEW)), device_id_type=MESH
        )
    pl.semaphore_wait(barrier, NCELL - 1 + NVIEW - 1)

    @pl.loop(1, NCELL, unroll=3)
    def _(i):
        o = cell_peer(i, z, y)
        pltpu.make_async_remote_copy(
            src_ref=grad_ref.at[o],
            dst_ref=rx.at[c],
            send_sem=send_sem,
            recv_sem=recv_sem,
            device_id=(o, v),
            device_id_type=MESH,
        ).start()

    pltpu.make_async_copy(grad_ref.at[c], rx.at[c], recv_sem).start()

    ids = jnp.concatenate([ids_ref[0:1, :], ids_ref[1:2, :]], axis=1)
    block = lax.broadcasted_iota(jnp.int32, (NBLOCK, CAP * NCELL), 0)
    chosen = jnp.where(block == ids, 1.0, 0.0).astype(F32)
    row = jnp.minimum(v, COMP - 1)
    level = lax.broadcasted_iota(jnp.int32, (COMP, BLOCK), 0)
    for b in range(NBLOCK):
        lanes = pl.ds(b * BLOCK, BLOCK)
        for i, ref in enumerate((params_ref, first_ref, second_ref)):
            only = jnp.where(level == row, ref[:, lanes], 0.0)
            mine[i, pl.ds(b, 1), :] = jnp.sum(only, axis=0, keepdims=True)

    pltpu.make_async_copy(grad_ref, rx, recv_sem).wait()

    for p in range(COMP):
        values = jnp.concatenate([rx[:, j, p, :] for j in range(CAP)], axis=0)
        spread[p] = jnp.dot(chosen, values, precision=HIGHEST, preferred_element_type=F32)

    def part(i):
        w = lax.rem(v + i, NVIEW)
        return w, pltpu.make_async_remote_copy(
            src_ref=spread.at[jnp.minimum(w, COMP - 1)],
            dst_ref=shares.at[v],
            send_sem=part_send.at[i],
            recv_sem=part_recv.at[v],
            device_id=(c, w),
            device_id_type=MESH,
        )

    def arrived(buffer, sem, s):
        return pltpu.make_async_copy(buffer.at[s], buffer.at[s], sem.at[s])

    for i in range(1, NVIEW):
        w, copy = part(i)
        pl.when(w < COMP)(copy.start)

    def send_row(i):
        return pltpu.make_async_remote_copy(
            src_ref=rows.at[row],
            dst_ref=rows.at[row],
            send_sem=row_send.at[i],
            recv_sem=row_recv.at[row],
            device_id=(c, lax.rem(v + i, NVIEW)),
            device_id_type=MESH,
        )

    @pl.when(v < COMP)
    def _():
        for s in range(NVIEW):
            pl.when(v != s)(arrived(shares, part_recv, s).wait)
        shares[v] = spread[row]
        grad = shares[0]
        for s in range(1, NVIEW):
            grad = grad + shares[s]
        one = BETA_ONE * mine[1] + (1.0 - BETA_ONE) * grad
        two = BETA_TWO * mine[2] + (1.0 - BETA_TWO) * grad * grad
        fix_one = 1.0 - BETA_ONE**FIRST_STEP
        fix_two = 1.0 - BETA_TWO**FIRST_STEP
        rows[row] = mine[0] - LEARN_RATE * (one / fix_one) / (jnp.sqrt(two / fix_two) + ADAM_EPS)
        for i in range(1, NVIEW):
            send_row(i).start()

    for p in range(COMP):
        pl.when(v != p)(arrived(rows, row_recv, p).wait)
        for b in range(NBLOCK):
            out_ref[pl.ds(p, 1), pl.ds(b * BLOCK, BLOCK)] = rows[p, pl.ds(b, 1), :]

    rest = pl.ds(0, NCELL - 1)
    pltpu.make_async_copy(grad_ref.at[rest], rx.at[rest], send_sem).wait()
    for i in range(1, NVIEW):
        w, copy = part(i)
        pl.when(w < COMP)(copy.wait_send)

    @pl.when(v < COMP)
    def _():
        for i in range(1, NVIEW):
            send_row(i).wait_send()


def shards(
    params, first_moment, second_moment, camera, slot_block, slot_anchor, tile_items, target
):
    vmem = pl.BlockSpec(memory_space=pltpu.VMEM)
    smem = pl.BlockSpec(memory_space=pltpu.SMEM)
    ids = jnp.transpose(slot_block[0, 0, 0], (1, 0))
    anchors = jnp.transpose(slot_anchor[0, 0, 0], (0, 2, 1)).reshape(2 * CAP, NCELL)
    items = jnp.transpose(tile_items[0, 0], (1, 0))
    goals = jnp.transpose(target[0, 0], (1, 0, 2))
    message = (NCELL, CAP, COMP, BLOCK)
    dma = pltpu.SemaphoreType.DMA
    arrived = pl.pallas_call(
        send_blocks,
        out_shape=jax.ShapeDtypeStruct(message, F32),
        in_specs=[smem, smem, smem, vmem],
        out_specs=vmem,
        scratch_shapes=[
            pltpu.VMEM((1 + NBLOCK, COMP, BLOCK), F32),
            pltpu.VMEM(message, F32),
            dma,
            dma,
        ],
        compiler_params=pltpu.CompilerParams(
            collective_id=0, has_side_effects=True, vmem_limit_bytes=24 << 20
        ),
    )(camera[0], ids, anchors, params)
    item_grads, losses = pl.pallas_call(
        render,
        out_shape=[
            jax.ShapeDtypeStruct(message, F32),
            jax.ShapeDtypeStruct((1, TILES), F32),
        ],
        in_specs=[smem, smem, vmem, vmem, vmem],
        out_specs=[vmem, vmem],
        scratch_shapes=[
            pltpu.VMEM((TILES * DEPTH, BLOCK, PIX), F32),
            pltpu.VMEM((5, DEPTH, TILES, PIX), F32),
            pltpu.VMEM((5, DEPTH, 2, TILES, 128), F32),
        ],
        compiler_params=pltpu.CompilerParams(vmem_limit_bytes=24 << 20),
    )(camera[0], items, arrived, goals, blur_matrix())
    share = (NVIEW, NBLOCK, BLOCK)
    new_params = pl.pallas_call(
        return_and_step,
        out_shape=jax.ShapeDtypeStruct((COMP, NBLOCK * BLOCK), F32),
        in_specs=[vmem] * 5,
        out_specs=vmem,
        scratch_shapes=[
            pltpu.VMEM(message, F32),
            pltpu.VMEM((COMP, NBLOCK, BLOCK), F32),
            pltpu.VMEM(share, F32),
            pltpu.VMEM((COMP, NBLOCK, BLOCK), F32),
            pltpu.VMEM((3, NBLOCK, BLOCK), F32),
            dma,
            dma,
            dma((NVIEW,)),
            dma((NVIEW,)),
            dma((NVIEW,)),
            dma((NVIEW,)),
        ],
        compiler_params=pltpu.CompilerParams(
            collective_id=1, has_side_effects=True, vmem_limit_bytes=24 << 20
        ),
    )(item_grads, ids, params, first_moment, second_moment)
    return (new_params, losses.reshape(1, 1, TILES))


def solution(mesh):
    placed = (
        P(None, "cell"),
        P(None, "cell"),
        P(None, "cell"),
        P(None, "view", None),
        P(None, "view", "cell", None, None),
        P(None, "view", "cell", None, None, None),
        P(None, "view", "cell", None),
        P(None, "view", "cell", None, None),
    )
    return jax.shard_map(
        shards,
        mesh=mesh,
        in_specs=placed,
        out_specs=(P(None, "cell"), P(None, "view", "cell")),
        check_vma=False,
    )
```

time: 198 us -> 154 us (0.78)
  Pallas kernels: 0 us -> 151 us
  waiting for transfers between devices: 59.4 us -> 0 us
  starting transfers between devices: 36.3 us -> 0 us
  other arithmetic: 35.6 us -> 0 us
  matrix products: 26.9 us -> 0 us
  local copies, waits for them, and re-layouts: 19.9 us -> 2.37 us
  blocking collectives: 9.95 us -> 0 us
  loops' own time: 6.84 us -> 0 us
    pallas_call x0 -> x3, Pallas kernels: none -> 151 us  [the longest x1 61.2 us: shards(): pl.pallas_call(render, out_shape=[jax.ShapeDtypeStruct(message, F32), jax...]
    all_to_all x3 -> x0, waiting for transfers between devices: 59.4 us -> none  [the longest x1 26.6 us: sent_together(): lax.all_to_all(both, axis, split_axis=split_dim, concat_axis=concat_dim,...]
    all_to_all x3 -> x0, starting transfers between devices: 36.3 us -> none  [the longest x1 19.4 us: sent_together(): lax.all_to_all(both, axis, split_axis=split_dim, concat_axis=concat_dim,...]
    dot_general x41 -> x0, matrix products: 26.9 us -> none  [the longest x24 22.9 us: splat_block(): weighted = jnp.einsum('ncg,ngp->ncp', colours, alphas, precision=highest)]
    add_any x24 -> x0, other arithmetic: 15.4 us -> none  [the longest x8 10.1 us: splat_block(): (1.0 + camera_row[0]) * pos_x + camera_row[1] * pos_y + anchors[:, 0:1]]
    mul x104 -> x0, other arithmetic: 11.2 us -> none  [the longest x24 10.3 us: splat_block(): opacity = opacity_cap * jax.nn.sigmoid(block_params[:, 3])]
    all_to_all x1 -> x0, blocking collectives: 9.95 us -> none  [copy_for_each(): lax.all_to_all(jnp.broadcast_to(array[None], (count, *array.shape)), axis...]
    another operation x1 -> x0, loops' own time: 6.84 us -> none  [in_groups(): results = lax.map(lambda pieces: function(*pieces), shaped)]
  transfers between devices with their start and end apart: 3 -> 0, of which waited for: 3 -> 0; matrix products, arithmetic and copies ran while one was open for 1% -> 0% of each run, Pallas kernels for 0% -> 0%
where the time goes in v1:
time: 154 us
  Pallas kernels  151 us (98%)
  local copies, waits for them, and re-layouts  2.37 us (2%)
    pallas_call x1, Pallas kernels, shards(): pl.pallas_call(render, out_shape=[jax.ShapeDtypeStruct(message, F32), jax...  61.2 us
    pallas_call x1, Pallas kernels, shards(): pl.pallas_call(return_and_step, out_shape=jax.ShapeDtypeStruct((COMP, NBL...  54.2 us
    pallas_call x1, Pallas kernels, shards(): pl.pallas_call(send_blocks, out_shape=jax.ShapeDtypeStruct(message, F32),...  35.4 us

profile of v1, /device:TPU:1, one launch (start us, length us, event | category | flops | bytes accessed | tf_op | source)
XLA Modules:
  0.0 153.9 jit_solution(8534036686102915583)
XLA Ops:
  0.6 0.0 copy-start.7
  0.6 0.0 copy-start.6
  0.7 0.0 copy-start.9
  0.7 0.7 copy-done.7
  1.3 0.0 copy-done.6
  1.3 0.0 copy-done.9
  1.3 0.0 copy-start
  1.3 0.9 copy-done
  2.3 0.0 copy-start.4
  2.3 0.0 copy-start.5
  2.3 0.0 copy-start.8
  2.3 35.4 %shard_map.104.rx_ref = f32[64,2,7,128]{3,2,1,0:T(8,128)S(1)} custom-call(f32[1,4]{1,0:T(1,128)S(1)} %bitcast.21, s32[2,64]{1,0:T(2,128)S(1)} %bitcast.17, f32[4,64]{1,0:T(4,128)S(1)} %bitcast.19, f32[7,8192]{1,0:T(8,128)S(1)} %copy-done), custom_call_target="tpu_custom_call" | custom-call | tf_op jit(solution)/shard_map/pallas_call | solution.py:430
  37.7 0.0 copy-done.4
  37.7 0.0 copy-done.5
  37.7 0.0 copy-done.8
  37.7 0.0 copy-start.1
  37.7 0.0 copy-start.2
  37.7 0.0 copy-start.3
  37.7 61.2 %shard_map.105 = (f32[64,2,7,128]{3,2,1,0:T(8,128)S(1)}, f32[1,8]{1,0:T(1,128)}) custom-call(f32[1,4]{1,0:T(1,128)S(1)} %bitcast.22, s32[4,8]{1,0:T(4,128)S(1)} %bitcast.20, f32[64,2,7,128]{3,2,1,0:T(8,128)S(1)} %shard_map.104.rx_ref, f32[3,8,256]{2,1,0:T(8,128)S(1)} %bitcast.16, f32[256,256]{1,0:T(8,128)S(1)} %copy-done.4), custom_call_target="tpu_custom_call" | custom-call | tf_op jit(solution)/shard_map/pallas_call | solution.py:445
  99.0 0.0 copy-done.1
  99.0 0.0 copy-done.2
  99.0 0.0 copy-done.3
  99.0 54.2 %shard_map.106 = f32[7,8192]{1,0:T(8,128)S(1)} custom-call(f32[64,2,7,128]{3,2,1,0:T(8,128)S(1)} %get-tuple-element.4.grad_ref, s32[2,64]{1,0:T(2,128)S(1)} %bitcast.18, f32[7,8192]{1,0:T(8,128)S(1)} %copy-done.1, f32[7,8192]{1,0:T(8,128)S(1)} %copy-done.2, f32[7,8192]{1,0:T(8,128)S(1)} %copy-done.3), custom_call_target="tpu_custom_call" | custom-call | tf_op jit(solution)/shard_map/pallas_call | solution.py:461
  153.2 0.7 copy.12
Async XLA Ops:
  0.6 0.7 copy-start.7
  0.6 0.7 copy-start.6
  0.7 0.7 copy-start.9
  1.3 1.0 copy-start
  2.3 35.4 %copy-start.4 = (f32[256,256]{1,0:T(8,128)S(1)}, f32[256,256]{1,0:T(8,128)}, u32[]{:S(2)}) copy-start(f32[256,256]{1,0:T(8,128)} %constant.2.clone.blur_ref) | copy-start | bytes 786436
  2.3 35.4 %copy-start.5 = (f32[1,1,8,3,256]{4,2,3,1,0:T(8,128)S(1)}, f32[1,1,8,3,256]{4,2,3,1,0:T(8,128)}, u32[]{:S(2)}) copy-start(f32[1,1,8,3,256]{4,2,3,1,0:T(8,128)} %param.16) | copy-start | bytes 73732
  2.3 35.4 %copy-start.8 = (s32[1,1,8,4]{2,3,1,0:T(4,128)S(1)}, s32[1,1,8,4]{2,3,1,0:T(4,128)}, u32[]{:S(2)}) copy-start(s32[1,1,8,4]{2,3,1,0:T(4,128)} %param.15) | copy-start | bytes 388
  37.7 61.3 %copy-start.1 = (f32[7,8192]{1,0:T(8,128)S(1)}, f32[7,8192]{1,0:T(8,128)}, u32[]{:S(2)}) copy-start(f32[7,8192]{1,0:T(8,128)} %params_ref.3) | copy-start | bytes 688132
  37.7 61.3 %copy-start.2 = (f32[7,8192]{1,0:T(8,128)S(1)}, f32[7,8192]{1,0:T(8,128)}, u32[]{:S(2)}) copy-start(f32[7,8192]{1,0:T(8,128)} %first_ref.1) | copy-start | bytes 688132
  37.7 61.3 %copy-start.3 = (f32[7,8192]{1,0:T(8,128)S(1)}, f32[7,8192]{1,0:T(8,128)}, u32[]{:S(2)}) copy-start(f32[7,8192]{1,0:T(8,128)} %second_ref.1) | copy-start | bytes 688132

commit v2 on v1

--- a/solution.py
+++ b/solution.py
@@ -122,6 +122,20 @@
     grid_y = [((lane >> 4).astype(F32) + (0.5 + half * 8)) / SIDE for half in range(2)]
     halves = [pl.ds(0, 128), pl.ds(128, 128)]
 
+    def split(x, narrow=False):
+        parts = []
+        for _ in range(3):
+            part = x.astype(jnp.bfloat16)
+            parts.append(part if narrow else part.astype(F32))
+            x = x - part.astype(F32)
+        return parts
+
+    def tinted(tile):
+        shifted = jnp.concatenate([tile[4:7], tile[0:5]], axis=0)
+        return jnp.where(level == 3, 1.0, jnp.where(level < 3, shifted, 0.0))
+
+    level256 = lax.broadcasted_iota(jnp.int32, (GROUP, PIX), 0)
+
     def columns(e):
         tile = rx_ref[e >> 1, e & 1]
         return tile, jnp.transpose(jnp.concatenate([tile, jnp.zeros((1, BLOCK), F32)], axis=0))
@@ -132,12 +146,11 @@
     @pl.loop(0, TILES)
     def _(t):
         for k in range(DEPTH):
-            _, cols = columns(items_ref[k, t])
+            tile, cols = columns(items_ref[k, t])
             slot = t * DEPTH + k
             clear = [jnp.ones((GROUP, 128), F32) for _ in range(2)]
-            sums = [[jnp.zeros((GROUP, 128), F32) for _ in range(4)] for _ in range(2)]
             for g in range(BLOCK // GROUP):
-                u, w, inverse, opacity, c0, c1, c2 = (spread(cols, g, i) for i in range(COMP))
+                u, w, inverse, opacity = (spread(cols, g, i) for i in range(4))
                 dx = grid_x - u
                 dx2 = dx * dx
                 for half in range(2):
@@ -145,21 +158,20 @@
                     alpha = opacity * jnp.exp(-(dx2 + dy * dy) * inverse)
                     alphas[slot, pl.ds(g * GROUP, GROUP), halves[half]] = alpha
                     clear[half] = clear[half] * (1.0 - alpha)
-                    s = sums[half]
-                    s[0] = s[0] + alpha
-                    s[1] = s[1] + c0 * alpha
-                    s[2] = s[2] + c1 * alpha
-                    s[3] = s[3] + c2 * alpha
+            alpha = alphas[slot]
+            first = alpha.astype(jnp.bfloat16)
+            second = (alpha - first.astype(F32)).astype(jnp.bfloat16)
+            wh, wm, _ = split(tinted(tile))
+            both = jnp.dot(jnp.concatenate([wh, wm], axis=0).astype(jnp.bfloat16), first, preferred_element_type=F32)
+            rest = jnp.dot(jnp.concatenate([wh, wh], axis=0).astype(jnp.bfloat16), second, preferred_element_type=F32)
+            sums = both[0:8] + both[8:16] + rest[0:8]
             for half in range(2):
                 p = clear[half]
                 for step in (4, 2, 1):
                     p = p * pltpu.roll(p, step, 0)
-                for i, whole in enumerate([p, *sums[half]]):
-                    if i:
-                        whole = jnp.sum(whole, axis=0, keepdims=True)
-                    merged[i, k, :, halves[half]] = jnp.where(
-                        level == t, whole, merged[i, k, :, halves[half]]
-                    )
+                merged[0, k, :, halves[half]] = jnp.where(level == t, p, merged[0, k, :, halves[half]])
+            for i in range(4):
+                merged[1 + i, k] = jnp.where(level256 == t, sums[3 if i == 0 else i - 1 : 4 if i == 0 else i], merged[1 + i, k])
 
     fronts = [jnp.ones((TILES, PIX), F32)]
     images = [jnp.zeros((TILES, PIX), F32) for _ in range(3)]
@@ -222,6 +234,7 @@
     )
     g_ch = [g_image[ch * TILES : (ch + 1) * TILES] for ch in range(3)]
     g_front = jnp.zeros((TILES, PIX), F32)
+    back[...] = jnp.zeros((TILES, DEPTH, 8, PIX), F32)
     for k in reversed(range(DEPTH)):
         transmit, total = merged[0, k], merged[1, k]
         floor = jnp.maximum(total, WEIGHT_FLOOR)
@@ -232,9 +245,22 @@
         share = jnp.where(total > WEIGHT_FLOOR, 1.0, jnp.where(total == WEIGHT_FLOOR, 0.5, 0.0))
         ways = [fronts[k] * g_ch[ch] * shade for ch in range(3)]
         for i, way in enumerate([*ways, -share * lit * shade, g_transmit * transmit]):
-            for half in range(2):
-                back[i, k, half] = way[:, half * 128 : (half + 1) * 128]
+            for at in range(TILES):
+                back[at, k, i : i + 1, :] = way[at : at + 1]
         g_front = sum(g_ch[ch] * colours[k][ch] for ch in range(3)) + transmit * g_front
+
+    def turned(rows, x):
+        return lax.dot_general(rows, x, (((1,), (1,)), ((), ())), preferred_element_type=F32)
+
+    def newton(x):
+        r = pl.reciprocal(x, approx=True)
+        return r * (2.0 - x * r)
+
+    place = lax.broadcasted_iota(jnp.int32, (16, PIX), 1)
+    kind = lax.broadcasted_iota(jnp.int32, (16, PIX), 0)
+    at_x = ((place & (SIDE - 1)).astype(F32) - 7.5) / SIDE
+    at_y = ((place >> 4).astype(F32) - 7.5) / SIDE
+    basis = jnp.where(kind == 0, 1.0, jnp.where(kind == 1, at_x, jnp.where(kind == 2, at_y, jnp.where(kind == 3, at_x * at_x + at_y * at_y, 0.0)))).astype(jnp.bfloat16)
 
     @pl.loop(0, NCELL)
     def _(i):
@@ -246,47 +272,27 @@
     def _(t):
         for k in range(DEPTH):
             e = items_ref[k, t]
-            tile, cols = columns(e)
+            tile = rx_ref[e >> 1, e & 1]
             slot = t * DEPTH + k
-            rays = [
-                [
-                    jnp.broadcast_to(back[i, k, half, pl.ds(t, 1), :], (GROUP, 128))
-                    for half in range(2)
-                ]
-                for i in range(5)
-            ]
-            pieces = []
-            for g in range(BLOCK // GROUP):
-                u, w, _, _, c0, c1, c2 = (spread(cols, g, i) for i in range(COMP))
-                dx = grid_x - u
-                q_sum = qy = qr = None
-                tints = [None] * 3
-                for half in range(2):
-                    alpha = alphas[slot, pl.ds(g * GROUP, GROUP), halves[half]]
-                    dy = grid_y[half] - w
-                    slope = (
-                        c0 * rays[0][half]
-                        + c1 * rays[1][half]
-                        + c2 * rays[2][half]
-                        + rays[3][half]
-                        - rays[4][half] / (1.0 - alpha)
-                    )
-                    q = slope * alpha
-                    qd = q * dy
-                    parts = [q, qd, qd * dy] + [rays[ch][half] * alpha for ch in range(3)]
-                    if half == 0:
-                        q_sum, qy, qr, *tints = parts
-                    else:
-                        q_sum, qy, qr = q_sum + parts[0], qy + parts[1], qr + parts[2]
-                        tints = [tints[ch] + parts[3 + ch] for ch in range(3)]
-                qx = q_sum * dx
-                qr = qr + qx * dx
-                lane8 = lax.broadcasted_iota(jnp.int32, (GROUP, GROUP), 1)
-                piece = jnp.zeros((GROUP, GROUP), F32)
-                for i, value in enumerate([qx, qy, qr, q_sum, *tints]):
-                    piece = jnp.where(lane8 == i, jnp.sum(value, axis=1, keepdims=True), piece)
-                pieces.append(piece)
-            sums = jnp.transpose(jnp.concatenate(pieces, axis=0))
+            rays = back[t, k]
+            alpha = alphas[slot]
+            ah, am, al = split(tinted(tile))
+            rh, rm, rl = split(rays)
+            slope = lax.dot_general(
+                jnp.concatenate([ah, ah, am, am, ah, al], axis=0).astype(jnp.bfloat16),
+                jnp.concatenate([rh, rm, rh, rm, rl, rh], axis=0).astype(jnp.bfloat16),
+                (((0,), (0,)), ((), ())), preferred_element_type=F32)
+            clear = 1.0 - alpha
+            inv = newton(clear)
+            q = (slope - rays[4:5] * inv) * alpha
+            moments = sum(turned(basis, part) for part in split(q, True))
+            first = alpha.astype(jnp.bfloat16)
+            second = (alpha - first.astype(F32)).astype(jnp.bfloat16)
+            both = turned(jnp.concatenate([rh, rm], axis=0).astype(jnp.bfloat16), first)
+            tints = both[0:3] + both[8:11] + turned(jnp.concatenate([rh, rh], axis=0).astype(jnp.bfloat16), second)[0:3]
+            m0, mx, my, mr = (moments[i:i+1] for i in range(4))
+            cu, cw = tile[0:1] - 0.5, tile[1:2] - 0.5
+            sums = jnp.concatenate([mx - cu * m0, my - cw * m0, mr - 2.0 * (cu * mx + cw * my) + (cu * cu + cw * cw) * m0, m0, tints], axis=0)
             twice = 2.0 * tile[2:3]
             du = twice * sums[0:1]
             dw = twice * sums[1:2]
@@ -453,7 +459,7 @@
         scratch_shapes=[
             pltpu.VMEM((TILES * DEPTH, BLOCK, PIX), F32),
             pltpu.VMEM((5, DEPTH, TILES, PIX), F32),
-            pltpu.VMEM((5, DEPTH, 2, TILES, 128), F32),
+            pltpu.VMEM((TILES, DEPTH, 8, PIX), F32),
         ],
         compiler_params=pltpu.CompilerParams(vmem_limit_bytes=24 << 20),
     )(camera[0], items, arrived, goals, blur_matrix())

time: 154 us -> 107 us (0.69)
  Pallas kernels: 151 us -> 104 us
    pallas_call x1, Pallas kernels: 61.2 us -> 14.4 us  [shards(): pl.pallas_call(render, out_shape=[jax.ShapeDtypeStruct(message, F32), jax...]
where the time goes in v2:
time: 107 us
  Pallas kernels  104 us (97%)
  local copies, waits for them, and re-layouts  2.36 us (2%)
    pallas_call x1, Pallas kernels, shards(): pl.pallas_call(return_and_step, out_shape=jax.ShapeDtypeStruct((COMP, NBL...  54.2 us
    pallas_call x1, Pallas kernels, shards(): pl.pallas_call(send_blocks, out_shape=jax.ShapeDtypeStruct(message, F32),...  35.4 us
    pallas_call x1, Pallas kernels, shards(): pl.pallas_call(render, out_shape=[jax.ShapeDtypeStruct(message, F32), jax...  14.4 us
    unnamed x21, local copies, waits for them, and re-layouts  2.36 us

profile of v2, /device:TPU:1, one launch (start us, length us, event | category | flops | bytes accessed | tf_op | source)
XLA Modules:
  0.0 107.1 jit_solution(12950341182780889545)
XLA Ops:
  0.6 0.0 copy-start.7
  0.6 0.0 copy-start.6
  0.7 0.0 copy-start.9
  0.7 0.7 copy-done.7
  1.3 0.0 copy-done.6
  1.3 0.0 copy-done.9
  1.3 0.0 copy-start
  1.3 0.9 copy-done
  2.3 0.0 copy-start.4
  2.3 0.0 copy-start.5
  2.3 0.0 copy-start.8
  2.3 35.4 %shard_map.104.rx_ref = f32[64,2,7,128]{3,2,1,0:T(8,128)S(1)} custom-call(f32[1,4]{1,0:T(1,128)S(1)} %bitcast.21, s32[2,64]{1,0:T(2,128)S(1)} %bitcast.17, f32[4,64]{1,0:T(4,128)S(1)} %bitcast.19, f32[7,8192]{1,0:T(8,128)S(1)} %copy-done), custom_call_target="tpu_custom_call" | custom-call | tf_op jit(solution)/shard_map/pallas_call | solution.py:436
  37.7 0.0 copy-done.4
  37.7 0.0 copy-done.5
  37.7 0.0 copy-done.8
  37.7 0.0 copy-start.1
  37.7 0.0 copy-start.2
  37.7 0.0 copy-start.3
  37.7 14.4 %shard_map.105 = (f32[64,2,7,128]{3,2,1,0:T(8,128)S(1)}, f32[1,8]{1,0:T(1,128)}) custom-call(f32[1,4]{1,0:T(1,128)S(1)} %bitcast.22, s32[4,8]{1,0:T(4,128)S(1)} %bitcast.20, f32[64,2,7,128]{3,2,1,0:T(8,128)S(1)} %shard_map.104.rx_ref, f32[3,8,256]{2,1,0:T(8,128)S(1)} %bitcast.16, f32[256,256]{1,0:T(8,128)S(1)} %copy-done.4), custom_call_target="tpu_custom_call" | custom-call | tf_op jit(solution)/shard_map/pallas_call | solution.py:451
  52.1 0.0 copy-done.1
  52.1 0.0 copy-done.2
  52.2 0.0 copy-done.3
  52.2 54.2 %shard_map.106 = f32[7,8192]{1,0:T(8,128)S(1)} custom-call(f32[64,2,7,128]{3,2,1,0:T(8,128)S(1)} %get-tuple-element.4.grad_ref, s32[2,64]{1,0:T(2,128)S(1)} %bitcast.18, f32[7,8192]{1,0:T(8,128)S(1)} %copy-done.1, f32[7,8192]{1,0:T(8,128)S(1)} %copy-done.2, f32[7,8192]{1,0:T(8,128)S(1)} %copy-done.3), custom_call_target="tpu_custom_call" | custom-call | tf_op jit(solution)/shard_map/pallas_call | solution.py:467
  106.4 0.7 copy.12
Async XLA Ops:
  0.6 0.7 copy-start.7
  0.6 0.7 copy-start.6
  0.7 0.7 copy-start.9
  1.3 1.0 copy-start
  2.3 35.4 %copy-start.4 = (f32[256,256]{1,0:T(8,128)S(1)}, f32[256,256]{1,0:T(8,128)}, u32[]{:S(2)}) copy-start(f32[256,256]{1,0:T(8,128)} %constant.2.clone.blur_ref) | copy-start | bytes 786436
  2.3 35.4 %copy-start.5 = (f32[1,1,8,3,256]{4,2,3,1,0:T(8,128)S(1)}, f32[1,1,8,3,256]{4,2,3,1,0:T(8,128)}, u32[]{:S(2)}) copy-start(f32[1,1,8,3,256]{4,2,3,1,0:T(8,128)} %param.16) | copy-start | bytes 73732
  2.3 35.4 %copy-start.8 = (s32[1,1,8,4]{2,3,1,0:T(4,128)S(1)}, s32[1,1,8,4]{2,3,1,0:T(4,128)}, u32[]{:S(2)}) copy-start(s32[1,1,8,4]{2,3,1,0:T(4,128)} %param.15) | copy-start | bytes 388
  37.7 14.4 %copy-start.1 = (f32[7,8192]{1,0:T(8,128)S(1)}, f32[7,8192]{1,0:T(8,128)}, u32[]{:S(2)}) copy-start(f32[7,8192]{1,0:T(8,128)} %params_ref.3) | copy-start | bytes 688132
  37.7 14.4 %copy-start.2 = (f32[7,8192]{1,0:T(8,128)S(1)}, f32[7,8192]{1,0:T(8,128)}, u32[]{:S(2)}) copy-start(f32[7,8192]{1,0:T(8,128)} %first_ref.1) | copy-start | bytes 688132
  37.7 14.4 %copy-start.3 = (f32[7,8192]{1,0:T(8,128)S(1)}, f32[7,8192]{1,0:T(8,128)}, u32[]{:S(2)}) copy-start(f32[7,8192]{1,0:T(8,128)} %second_ref.1) | copy-start | bytes 688132

commit v3 on v2

v3 whole, which is shorter than its diff:
```python
import jax
import jax.numpy as jnp
import numpy as np
from jax import lax
from jax.experimental import pallas as pl
from jax.experimental.pallas import tpu as pltpu
from jax.sharding import PartitionSpec as P

SIDE = 16
PIX = 256
BLOCK = 128
COMP = 7
TAPS = 11
DEPTH = 4
TILES = 8
NCELL = 64
NVIEW = 8
NBLOCK = 64
CAP = 2
NZ = 16
NY = 4
GROUP = 8

SSIM_WEIGHT = 0.2
STABLE_ONE = 0.0001
STABLE_TWO = 0.0009
LEARN_RATE = 0.1
BETA_ONE = 0.9
BETA_TWO = 0.999
ADAM_EPS = 1e-08
FIRST_STEP = 1
OPACITY_CAP = 0.1
WEIGHT_FLOOR = 0.5

F32 = jnp.float32
BF16 = jnp.bfloat16
MESH = pl.DeviceIdType.MESH
HIGHEST = lax.Precision.HIGHEST


def blur_matrix():
    offsets = np.arange(SIDE)[:, None] - np.arange(SIDE)[None, :]
    kernel = np.exp(-(offsets * offsets) / 4.5) * (np.abs(offsets) <= TAPS // 2)
    kernel = kernel / kernel.sum(axis=1, keepdims=True)
    return jnp.asarray(np.kron(kernel, kernel).T, F32)


def cell_peer(i, z, y):
    i = NCELL - 1 - i
    k = lax.div(i, NY)
    m = lax.div(k + 1, 2)
    dz = jnp.where(lax.rem(k, 2) == 1, m, NZ - m)
    return lax.rem(z + dz, NZ) * NY + lax.rem(y + lax.rem(i, NY), NY)


def split(x):
    parts = []
    for _ in range(3):
        part = x.astype(BF16)
        parts.append(part)
        x = x - part.astype(F32)
    return parts


def stack(parts):
    return jnp.concatenate([part.astype(F32) for part in parts], axis=0).astype(BF16)


def product(left, right, dims=((1,), (0,))):
    return lax.dot_general(left, right, (dims, ((), ())), preferred_element_type=F32)


def blurred(rows, table):
    return jnp.dot(rows, table, precision=HIGHEST, preferred_element_type=F32)


def level_of(shape):
    return lax.broadcasted_iota(jnp.int32, shape, 0)


def lane_of(shape):
    return lax.broadcasted_iota(jnp.int32, shape, 1)


def tinted(tile):
    level = level_of((GROUP, BLOCK))
    shifted = jnp.concatenate([tile[4:7], tile[0:5]], axis=0)
    return jnp.where(level == 3, 1.0, jnp.where(level < 3, shifted, 0.0))


def derive(params_ref, camera_ref, derived):
    q0, q1, q2, q3 = (camera_ref[0, i] for i in range(4))
    width = 1024
    derived[0] = jnp.zeros((COMP, BLOCK), F32)
    for part in range(NBLOCK * BLOCK // width):
        values = params_ref[:, pl.ds(part * width, width)]
        row = level_of(values.shape)
        logistic = 1.0 / (1.0 + jnp.exp(-values))
        inverse = 0.5 * jnp.exp(-2.0 * values)
        pos_x, pos_y = values[0:1], values[1:2]
        base_u = (1.0 + q0) * pos_x + q1 * pos_y
        base_w = q2 * pos_x + (1.0 + q3) * pos_y
        out = jnp.where(row == 3, OPACITY_CAP * logistic, logistic)
        out = jnp.where(row == 2, inverse, out)
        out = jnp.where(row == 1, base_w, out)
        out = jnp.where(row == 0, base_u, out)
        for i in range(width // BLOCK):
            derived[1 + part * (width // BLOCK) + i] = out[:, i * BLOCK : (i + 1) * BLOCK]


def forward(items_ref, rx, alphas, merged):
    lane = lane_of((GROUP, 128))
    level = level_of((GROUP, 128))
    level_wide = level_of((GROUP, PIX))
    grid_x = ((lane & (SIDE - 1)).astype(F32) + 0.5) / SIDE
    grid_y = [((lane >> 4).astype(F32) + (0.5 + half * 8)) / SIDE for half in range(2)]
    halves = [pl.ds(0, 128), pl.ds(128, 128)]

    @pl.loop(0, TILES)
    def _(t):
        for k in range(DEPTH):
            tile = rx[items_ref[k, t]]
            cols = jnp.transpose(jnp.concatenate([tile, jnp.zeros((1, BLOCK), F32)], axis=0))
            slot = t * DEPTH + k
            clear = [jnp.ones((GROUP, 128), F32) for _ in range(2)]
            for g in range(BLOCK // GROUP):
                rows = slice(g * GROUP, (g + 1) * GROUP)
                u, w, inverse, opacity = (
                    jnp.broadcast_to(cols[rows, i : i + 1], (GROUP, 128)) for i in range(4)
                )
                dx = grid_x - u
                dx2 = dx * dx
                for half in range(2):
                    dy = grid_y[half] - w
                    alpha = opacity * jnp.exp(-(dx2 + dy * dy) * inverse)
                    alphas[slot, pl.ds(g * GROUP, GROUP), halves[half]] = alpha
                    clear[half] = clear[half] * (1.0 - alpha)
            alpha = alphas[slot]
            first = alpha.astype(BF16)
            second = (alpha - first.astype(F32)).astype(BF16)
            wh, wm, _ = split(tinted(tile))
            both = product(stack([wh, wm]), first)
            rest = product(stack([wh, wh]), second)
            sums = both[0:8] + both[8:16] + rest[0:8]
            for half in range(2):
                p = clear[half]
                for step in (4, 2, 1):
                    p = p * pltpu.roll(p, step, 0)
                merged[0, k, :, halves[half]] = jnp.where(
                    level == t, p, merged[0, k, :, halves[half]]
                )
            for i, at in enumerate((3, 0, 1, 2)):
                merged[1 + i, k] = jnp.where(
                    level_wide == t, sums[at : at + 1], merged[1 + i, k]
                )


def compare(merged, goals, goal_blur, blur_ref, loss_ref, back):
    fronts = [jnp.ones((TILES, PIX), F32)]
    images = [jnp.zeros((TILES, PIX), F32) for _ in range(3)]
    colours = []
    for k in range(DEPTH):
        transmit, total = merged[0, k], merged[1, k]
        scale = (1.0 - transmit) / jnp.maximum(total, WEIGHT_FLOOR)
        shaded = [scale * merged[2 + ch, k] for ch in range(3)]
        images = [images[ch] + fronts[k] * shaded[ch] for ch in range(3)]
        colours.append(shaded)
        fronts.append(fronts[k] * transmit)

    a, b = jnp.concatenate(images, axis=0), goals
    rows = 3 * TILES
    table = blur_ref[...]
    mine = blurred(jnp.concatenate([a, a * a, a * b], axis=0), table)
    ma, saa, sab = (mine[i * rows : (i + 1) * rows] for i in range(3))
    mb, sbb = goal_blur[0:rows], goal_blur[rows:]
    va = saa - ma * ma
    vb = sbb - mb * mb
    cab = sab - ma * mb
    n1 = 2.0 * ma * mb + STABLE_ONE
    n2 = 2.0 * cab + STABLE_TWO
    d1 = ma * ma + mb * mb + STABLE_ONE
    d2 = va + vb + STABLE_TWO
    under = 1.0 / (d1 * d2)
    ssim = n1 * n2 * under
    apart = a - b
    values = (1.0 - SSIM_WEIGHT) * apart * apart + SSIM_WEIGHT * (1.0 - ssim)
    per_tile = values[0:TILES] + values[TILES : 2 * TILES] + values[2 * TILES :]
    count = 3.0 * PIX
    loss = jnp.sum(per_tile, axis=1, keepdims=True) / count
    square = (TILES, TILES)
    loss_ref[...] = jnp.sum(
        jnp.where(level_of(square) == lane_of(square), loss, 0.0), axis=0, keepdims=True
    )

    g_s = -SSIM_WEIGHT / count
    g_n1 = g_s * n2 * under
    g_n2 = g_s * n1 * under
    g_d1 = -g_s * ssim / d1
    g_d2 = -g_s * ssim / d2
    g_ab = 2.0 * g_n2
    g_ma = 2.0 * mb * g_n1 + 2.0 * ma * g_d1 - mb * g_ab - 2.0 * ma * g_d2
    backed = lax.dot_general(
        jnp.concatenate([g_ma, g_d2, g_ab], axis=0),
        table,
        (((1,), (1,)), ((), ())),
        precision=HIGHEST,
        preferred_element_type=F32,
    )
    g_image = (
        (2.0 * (1.0 - SSIM_WEIGHT) / count) * apart
        + backed[0:rows]
        + 2.0 * a * backed[rows : 2 * rows]
        + b * backed[2 * rows :]
    )
    g_ch = [g_image[ch * TILES : (ch + 1) * TILES] for ch in range(3)]
    g_front = jnp.zeros((TILES, PIX), F32)
    for k in reversed(range(DEPTH)):
        transmit, total = merged[0, k], merged[1, k]
        over = 1.0 / jnp.maximum(total, WEIGHT_FLOOR)
        shade = (1.0 - transmit) * over
        lit = sum(g_ch[ch] * merged[2 + ch, k] for ch in range(3)) * over * fronts[k]
        g_transmit = fronts[k] * g_front - lit
        share = jnp.where(total > WEIGHT_FLOOR, 1.0, jnp.where(total == WEIGHT_FLOOR, 0.5, 0.0))
        ways = [fronts[k] * g_ch[ch] * shade for ch in range(3)]
        for i, way in enumerate([*ways, -share * lit * shade, g_transmit * transmit]):
            for t in range(TILES):
                back[t, k, i : i + 1, :] = way[t : t + 1]
        g_front = sum(g_ch[ch] * colours[k][ch] for ch in range(3)) + transmit * g_front


def backward(camera_ref, items_ref, rx, alphas, back, item_grads):
    q0, q1, q2, q3 = (camera_ref[0, i] for i in range(4))
    place = lane_of((16, PIX))
    kind = level_of((16, PIX))
    at_x = ((place & (SIDE - 1)).astype(F32) - 7.5) / SIDE
    at_y = ((place >> 4).astype(F32) - 7.5) / SIDE
    basis = jnp.where(kind == 3, at_x * at_x + at_y * at_y, 0.0)
    basis = jnp.where(kind == 2, at_y, jnp.where(kind == 1, at_x, basis))
    basis = jnp.where(kind == 0, 1.0, basis).astype(BF16)
    along = ((1,), (1,))

    @pl.loop(0, TILES)
    def _(t):
        for k in range(DEPTH):
            tile = rx[items_ref[k, t]]
            slot = t * DEPTH + k
            rays = back[t, k]
            alpha = alphas[slot]
            ah, am, al = split(tinted(tile))
            rh, rm, rl = split(rays)
            slope = product(
                stack([ah, ah, am, am, ah, al]), stack([rh, rm, rh, rm, rl, rh]), ((0,), (0,))
            )
            q = (slope - rays[4:5] / (1.0 - alpha)) * alpha
            moments = sum(product(basis, part, along) for part in split(q))
            first = alpha.astype(BF16)
            second = (alpha - first.astype(F32)).astype(BF16)
            both = product(stack([rh, rm]), first, along)
            tints = both[0:3] + both[8:11] + product(stack([rh, rh]), second, along)[0:3]
            m0, mx, my, mr = (moments[i : i + 1] for i in range(4))
            cu, cw = tile[0:1] - 0.5, tile[1:2] - 0.5
            twice = 2.0 * tile[2:3]
            du = twice * (mx - cu * m0)
            dw = twice * (my - cw * m0)
            spread = mr - 2.0 * (cu * mx + cw * my) + (cu * cu + cw * cw) * m0
            tone = tile[4:7]
            item_grads[slot] = jnp.concatenate(
                [
                    (1.0 + q0) * du + q2 * dw,
                    q1 * du + (1.0 + q3) * dw,
                    twice * spread,
                    (1.0 - tile[3:4] / OPACITY_CAP) * m0,
                    tone * (1.0 - tone) * tints,
                    jnp.zeros((1, BLOCK), F32),
                ],
                axis=0,
            )


def step(
    camera_ref, ids_ref, anchor_ref, items_ref, ids_rows, items_rows, goal_ref, blur_ref,
    params_hbm, first_hbm, second_hbm, out_ref, loss_ref,
    params_ref, first_ref, second_ref, derived, tx, rx, alphas, merged, back, item_grads,
    grads, grads_rx, summed, shares, rows, mine,
    stage_sem, send_sem, recv_sem, back_send, back_recv, part_send, part_recv, row_send, row_recv,
):
    c = lax.axis_index("cell")
    v = lax.axis_index("view")
    z, y = lax.div(c, NY), lax.rem(c, NY)
    staged = [
        pltpu.make_async_copy(source, target, stage_sem.at[i])
        for i, (source, target) in enumerate(
            ((params_hbm, params_ref), (first_hbm, first_ref), (second_hbm, second_ref))
        )
    ]
    for copy in staged:
        copy.start()

    barrier = pltpu.get_barrier_semaphore()

    @pl.loop(0, NCELL - 1, unroll=9)
    def _(i):
        pl.semaphore_signal(
            barrier, inc=1, device_id=(cell_peer(i, z, y), v), device_id_type=MESH
        )

    for i in range(1, NVIEW):
        pl.semaphore_signal(
            barrier, inc=1, device_id=(c, lax.rem(v + i, NVIEW)), device_id_type=MESH
        )

    staged[0].wait()
    derive(params_ref, camera_ref, derived)
    pl.semaphore_wait(barrier, NCELL - 1 + NVIEW - 1)

    def pair(o):
        return pl.ds(o * CAP, CAP)

    def gather(o):
        row = level_of((COMP, BLOCK))
        for j in range(CAP):
            shift = jnp.where(
                row == 0, anchor_ref[j, o], jnp.where(row == 1, anchor_ref[CAP + j, o], 0.0)
            )
            tx[o * CAP + j] = derived[ids_ref[j, o] + 1] + shift

    @pl.loop(0, NCELL - 1, unroll=3)
    def _(i):
        o = cell_peer(i, z, y)
        gather(o)
        pltpu.make_async_remote_copy(
            src_ref=tx.at[pair(o)],
            dst_ref=rx.at[pair(c)],
            send_sem=send_sem,
            recv_sem=recv_sem,
            device_id=(o, v),
            device_id_type=MESH,
        ).start()

    gather(c)
    pltpu.make_async_copy(tx.at[pair(c)], rx.at[pair(c)], recv_sem).start()

    goals = jnp.concatenate([goal_ref[ch] for ch in range(3)], axis=0)
    goal_blur = blurred(jnp.concatenate([goals, goals * goals], axis=0), blur_ref[...])
    ids = jnp.concatenate([ids_rows[0:1, :], ids_rows[1:2, :]], axis=1)
    chosen = jnp.where(level_of((NBLOCK, CAP * NCELL)) == ids, 1.0, 0.0).astype(F32)
    row = jnp.minimum(v, COMP - 1)
    staged[1].wait()
    staged[2].wait()
    level = level_of((COMP, BLOCK))
    for b in range(NBLOCK):
        for i, ref in enumerate((params_ref, first_ref, second_ref)):
            only = jnp.where(level == row, ref[:, pl.ds(b * BLOCK, BLOCK)], 0.0)
            mine[i, pl.ds(b, 1), :] = jnp.sum(only, axis=0, keepdims=True)
    back[...] = jnp.zeros((TILES, DEPTH, GROUP, PIX), F32)
    merged[...] = jnp.zeros((5, DEPTH, TILES, PIX), F32)
    wide = (TILES, TILES * DEPTH * GROUP)
    place = lax.rem(lane_of((1, wide[1])), GROUP).astype(F32)
    for k in range(DEPTH):
        pick = jnp.where(lax.div(lane_of(wide), GROUP) == level_of(wide) * DEPTH + k, 1.0, 0.0)
        entries = jnp.broadcast_to(items_rows[k : k + 1, :].astype(F32), (TILES, TILES))
        place = place + GROUP * product(entries.astype(BF16), pick.astype(BF16))[0:1]

    pltpu.make_async_copy(tx, rx, recv_sem).wait()

    forward(items_ref, rx, alphas, merged)
    compare(merged, goals, goal_blur, blur_ref, loss_ref, back)
    backward(camera_ref, items_ref, rx, alphas, back, item_grads)

    parts = split(item_grads[...].reshape(TILES * DEPTH * GROUP, BLOCK))
    chunk = 256
    for part in range(NCELL * CAP * GROUP // chunk):
        at = (level_of((chunk, wide[1])) + part * chunk).astype(F32)
        spots = jnp.where(at == place, 1.0, 0.0).astype(BF16)
        found = sum(product(spots, x) for x in parts)
        for i in range(chunk // GROUP):
            slot = part * (chunk // GROUP) + i
            grads[slot // CAP, slot % CAP] = found[i * GROUP : i * GROUP + COMP]

    @pl.loop(0, NCELL - 1, unroll=9)
    def _(i):
        o = cell_peer(i, z, y)
        pltpu.make_async_remote_copy(
            src_ref=grads.at[o],
            dst_ref=grads_rx.at[c],
            send_sem=back_send,
            recv_sem=back_recv,
            device_id=(o, v),
            device_id_type=MESH,
        ).start()

    pltpu.make_async_copy(grads.at[c], grads_rx.at[c], back_recv).start()
    pltpu.make_async_copy(grads, grads_rx, back_recv).wait()

    for p in range(COMP):
        values = jnp.concatenate([grads_rx[:, j, p, :] for j in range(CAP)], axis=0)
        summed[p] = jnp.dot(chosen, values, precision=HIGHEST, preferred_element_type=F32)

    def part(i):
        w = lax.rem(v + i, NVIEW)
        return w, pltpu.make_async_remote_copy(
            src_ref=summed.at[jnp.minimum(w, COMP - 1)],
            dst_ref=shares.at[v],
            send_sem=part_send.at[i],
            recv_sem=part_recv.at[v],
            device_id=(c, w),
            device_id_type=MESH,
        )

    def arrived(buffer, sem, s):
        return pltpu.make_async_copy(buffer.at[s], buffer.at[s], sem.at[s])

    for i in range(1, NVIEW):
        w, copy = part(i)
        pl.when(w < COMP)(copy.start)

    def send_row(i):
        return pltpu.make_async_remote_copy(
            src_ref=rows.at[row],
            dst_ref=rows.at[row],
            send_sem=row_send.at[i],
            recv_sem=row_recv.at[row],
            device_id=(c, lax.rem(v + i, NVIEW)),
            device_id_type=MESH,
        )

    @pl.when(v < COMP)
    def _():
        for s in range(NVIEW):
            pl.when(v != s)(arrived(shares, part_recv, s).wait)
        shares[v] = summed[row]
        grad = shares[0]
        for s in range(1, NVIEW):
            grad = grad + shares[s]
        one = BETA_ONE * mine[1] + (1.0 - BETA_ONE) * grad
        two = BETA_TWO * mine[2] + (1.0 - BETA_TWO) * grad * grad
        fix_one = 1.0 - BETA_ONE**FIRST_STEP
        fix_two = 1.0 - BETA_TWO**FIRST_STEP
        rows[row] = mine[0] - LEARN_RATE * (one / fix_one) / (jnp.sqrt(two / fix_two) + ADAM_EPS)
        for i in range(1, NVIEW):
            send_row(i).start()

    for p in range(COMP):
        pl.when(v != p)(arrived(rows, row_recv, p).wait)
        for b in range(NBLOCK):
            out_ref[pl.ds(p, 1), pl.ds(b * BLOCK, BLOCK)] = rows[p, pl.ds(b, 1), :]

    rest = pl.ds(0, CAP * (NCELL - 1))
    pltpu.make_async_copy(tx.at[rest], rx.at[rest], send_sem).wait()
    rest = pl.ds(0, NCELL - 1)
    pltpu.make_async_copy(grads.at[rest], grads_rx.at[rest], back_send).wait()
    for i in range(1, NVIEW):
        w, copy = part(i)
        pl.when(w < COMP)(copy.wait_send)

    @pl.when(v < COMP)
    def _():
        for i in range(1, NVIEW):
            send_row(i).wait_send()


def shards(
    params, first_moment, second_moment, camera, slot_block, slot_anchor, tile_items, target
):
    vmem = pl.BlockSpec(memory_space=pltpu.VMEM)
    smem = pl.BlockSpec(memory_space=pltpu.SMEM)
    hbm = pl.BlockSpec(memory_space=pltpu.HBM)
    ids = jnp.transpose(slot_block[0, 0, 0], (1, 0))
    anchors = jnp.transpose(slot_anchor[0, 0, 0], (0, 2, 1)).reshape(2 * CAP, NCELL)
    items = jnp.transpose(tile_items[0, 0], (1, 0))
    goals = jnp.transpose(target[0, 0], (1, 0, 2))
    message = pltpu.VMEM((NCELL * CAP, COMP, BLOCK), F32)
    returned = pltpu.VMEM((NCELL, CAP, COMP, BLOCK), F32)
    whole = pltpu.VMEM((COMP, NBLOCK * BLOCK), F32)
    table = pltpu.VMEM((COMP, NBLOCK, BLOCK), F32)
    dma = pltpu.SemaphoreType.DMA
    new_params, losses = pl.pallas_call(
        step,
        out_shape=[
            jax.ShapeDtypeStruct((COMP, NBLOCK * BLOCK), F32),
            jax.ShapeDtypeStruct((1, TILES), F32),
        ],
        in_specs=[smem, smem, smem, smem, vmem, vmem, vmem, vmem, hbm, hbm, hbm],
        out_specs=[vmem, vmem],
        scratch_shapes=[
            whole,
            whole,
            whole,
            pltpu.VMEM((1 + NBLOCK, COMP, BLOCK), F32),
            message,
            message,
            pltpu.VMEM((TILES * DEPTH, BLOCK, PIX), F32),
            pltpu.VMEM((5, DEPTH, TILES, PIX), F32),
            pltpu.VMEM((TILES, DEPTH, GROUP, PIX), F32),
            pltpu.VMEM((TILES * DEPTH, GROUP, BLOCK), F32),
            returned,
            returned,
            table,
            pltpu.VMEM((NVIEW, NBLOCK, BLOCK), F32),
            table,
            pltpu.VMEM((3, NBLOCK, BLOCK), F32),
            dma((3,)),
            dma,
            dma,
            dma,
            dma,
            dma((NVIEW,)),
            dma((NVIEW,)),
            dma((NVIEW,)),
            dma((NVIEW,)),
        ],
        compiler_params=pltpu.CompilerParams(
            collective_id=0, has_side_effects=True, vmem_limit_bytes=32 << 20
        ),
    )(
        camera[0], ids, anchors, items, ids, items, goals, blur_matrix(),
        params, first_moment, second_moment,
    )
    return (new_params, losses.reshape(1, 1, TILES))


def solution(mesh):
    placed = (
        P(None, "cell"),
        P(None, "cell"),
        P(None, "cell"),
        P(None, "view", None),
        P(None, "view", "cell", None, None),
        P(None, "view", "cell", None, None, None),
        P(None, "view", "cell", None),
        P(None, "view", "cell", None, None),
    )
    return jax.shard_map(
        shards,
        mesh=mesh,
        in_specs=placed,
        out_specs=(P(None, "cell"), P(None, "view", "cell")),
        check_vma=False,
    )
```

time: 107 us -> 96.1 us (0.90)
  Pallas kernels: 104 us -> 88.7 us
  local copies, waits for them, and re-layouts: 2.36 us -> 6.43 us
    pallas_call x3 -> x1, Pallas kernels: 104 us -> 88.7 us  [shards(): pl.pallas_call(step, out_shape=[jax.ShapeDtypeStruct((COMP, NBLOCK * BLOC...]
    unnamed x21 -> x20, local copies, waits for them, and re-layouts: 2.36 us -> 6.43 us
where the time goes in v3:
time: 96.1 us; the launch traced here: 95.8 us
  Pallas kernels  88.7 us (92%)
  local copies, waits for them, and re-layouts  6.43 us (7%)
    pallas_call x1, Pallas kernels, shards(): pl.pallas_call(step, out_shape=[jax.ShapeDtypeStruct((COMP, NBLOCK * BLOC...  88.7 us
    unnamed x20, local copies, waits for them, and re-layouts  6.43 us

profile of v3, /device:TPU:1, one launch (start us, length us, event | category | flops | bytes accessed | tf_op | source)
XLA Modules:
  0.0 95.8 jit_solution(5554716856477118686)
XLA Ops:
  0.6 0.0 copy-start.7
  0.6 0.0 copy-start.5
  0.7 0.0 copy-start.6
  0.7 0.0 copy-start.8
  0.7 0.6 copy-done.7
  1.3 0.0 copy-done.5
  1.3 0.0 copy-done.6
  1.3 0.0 copy-done.8
  1.3 0.0 copy-start
  1.3 0.9 copy-done
  2.3 0.0 copy-start.1
  2.3 0.9 copy-done.1
  3.2 0.0 copy-start.2
  3.3 0.9 copy-done.2
  4.2 0.0 copy-start.3
  4.2 0.9 copy-done.3
  5.1 0.0 copy-start.4
  5.2 0.7 copy-done.4
  5.9 88.7 %shard_map.104 = (f32[7,8192]{1,0:T(8,128)S(1)}, f32[1,8]{1,0:T(1,128)S(1)}) custom-call(f32[1,4]{1,0:T(1,128)S(1)} %bitcast.22, s32[2,64]{1,0:T(2,128)S(1)} %bitcast.19, f32[4,64]{1,0:T(4,128)S(1)} %bitcast.21, s32[4,8]{1,0:T(4,128)S(1)} %bitcast.17, s32[2,64]{1,0:T(2,128)S(1)} %bitcast.20, s32[4,8]{1,0:T(4,128)S(1)} %bitcast.18, ...), custom_call_target="tpu_custom_call" | custom-call | tf_op jit(solution)/shard_map/pallas_call | solution.py:477
  94.6 0.7 copy.13
  95.3 0.5 copy.14
Async XLA Ops:
  0.6 0.7 copy-start.7
  0.6 0.7 copy-start.5
  0.7 0.7 copy-start.6
  0.7 0.7 copy-start.8
  1.3 1.0 copy-start
  2.3 0.9 copy-start.1
  3.2 0.9 copy-start.2
  4.2 0.9 copy-start.3
  5.1 0.7 copy-start.4

commit v4 on v3

--- a/solution.py
+++ b/solution.py
@@ -278,9 +278,9 @@
 
 
 def step(
-    camera_ref, ids_ref, anchor_ref, items_ref, ids_rows, items_rows, goal_ref, blur_ref,
+    camera_hbm, anchor_hbm, ids_hbm, items_hbm, goal_hbm, blur_hbm,
     params_hbm, first_hbm, second_hbm, out_ref, loss_ref,
-    params_ref, first_ref, second_ref, derived, tx, rx, alphas, merged, back, item_grads,
+    camera_ref, ids_ref, anchor_ref, items_ref, params_ref, first_ref, second_ref, ids_rows, items_rows, goal_ref, blur_ref, derived, tx, rx, alphas, merged, back, item_grads,
     grads, grads_rx, summed, shares, rows, mine,
     stage_sem, send_sem, recv_sem, back_send, back_recv, part_send, part_recv, row_send, row_recv,
 ):
@@ -290,7 +290,19 @@
     staged = [
         pltpu.make_async_copy(source, target, stage_sem.at[i])
         for i, (source, target) in enumerate(
-            ((params_hbm, params_ref), (first_hbm, first_ref), (second_hbm, second_ref))
+            (
+                (params_hbm, params_ref),
+                (first_hbm, first_ref),
+                (second_hbm, second_ref),
+                (ids_hbm, ids_rows),
+                (items_hbm, items_rows),
+                (goal_hbm, goal_ref),
+                (blur_hbm, blur_ref),
+                (camera_hbm, camera_ref),
+                (ids_hbm, ids_ref),
+                (anchor_hbm, anchor_ref),
+                (items_hbm, items_ref),
+            )
         )
     ]
     for copy in staged:
@@ -309,7 +321,8 @@
             barrier, inc=1, device_id=(c, lax.rem(v + i, NVIEW)), device_id_type=MESH
         )
 
-    staged[0].wait()
+    for i in (0, 7, 8, 9, 10):
+        staged[i].wait()
     derive(params_ref, camera_ref, derived)
     pl.semaphore_wait(barrier, NCELL - 1 + NVIEW - 1)
 
@@ -340,13 +353,13 @@
     gather(c)
     pltpu.make_async_copy(tx.at[pair(c)], rx.at[pair(c)], recv_sem).start()
 
+    for copy in staged[1:7]:
+        copy.wait()
     goals = jnp.concatenate([goal_ref[ch] for ch in range(3)], axis=0)
     goal_blur = blurred(jnp.concatenate([goals, goals * goals], axis=0), blur_ref[...])
     ids = jnp.concatenate([ids_rows[0:1, :], ids_rows[1:2, :]], axis=1)
     chosen = jnp.where(level_of((NBLOCK, CAP * NCELL)) == ids, 1.0, 0.0).astype(F32)
     row = jnp.minimum(v, COMP - 1)
-    staged[1].wait()
-    staged[2].wait()
     level = level_of((COMP, BLOCK))
     for b in range(NBLOCK):
         for i, ref in enumerate((params_ref, first_ref, second_ref)):
@@ -463,7 +476,6 @@
     params, first_moment, second_moment, camera, slot_block, slot_anchor, tile_items, target
 ):
     vmem = pl.BlockSpec(memory_space=pltpu.VMEM)
-    smem = pl.BlockSpec(memory_space=pltpu.SMEM)
     hbm = pl.BlockSpec(memory_space=pltpu.HBM)
     ids = jnp.transpose(slot_block[0, 0, 0], (1, 0))
     anchors = jnp.transpose(slot_anchor[0, 0, 0], (0, 2, 1)).reshape(2 * CAP, NCELL)
@@ -480,12 +492,20 @@
             jax.ShapeDtypeStruct((COMP, NBLOCK * BLOCK), F32),
             jax.ShapeDtypeStruct((1, TILES), F32),
         ],
-        in_specs=[smem, smem, smem, smem, vmem, vmem, vmem, vmem, hbm, hbm, hbm],
+        in_specs=[hbm] * 9,
         out_specs=[vmem, vmem],
         scratch_shapes=[
+            pltpu.SMEM((1, 4), F32),
+            pltpu.SMEM((CAP, NCELL), jnp.int32),
+            pltpu.SMEM((2 * CAP, NCELL), F32),
+            pltpu.SMEM((DEPTH, TILES), jnp.int32),
             whole,
             whole,
             whole,
+            pltpu.VMEM((CAP, NCELL), jnp.int32),
+            pltpu.VMEM((DEPTH, TILES), jnp.int32),
+            pltpu.VMEM((3, TILES, PIX), F32),
+            pltpu.VMEM((PIX, PIX), F32),
             pltpu.VMEM((1 + NBLOCK, COMP, BLOCK), F32),
             message,
             message,
@@ -499,7 +519,7 @@
             pltpu.VMEM((NVIEW, NBLOCK, BLOCK), F32),
             table,
             pltpu.VMEM((3, NBLOCK, BLOCK), F32),
-            dma((3,)),
+            dma((11,)),
             dma,
             dma,
             dma,
@@ -510,10 +530,10 @@
             dma((NVIEW,)),
         ],
         compiler_params=pltpu.CompilerParams(
-            collective_id=0, has_side_effects=True, vmem_limit_bytes=32 << 20
+            collective_id=0, has_side_effects=True, vmem_limit_bytes=56 << 20
         ),
     )(
-        camera[0], ids, anchors, items, ids, items, goals, blur_matrix(),
+        camera[0], anchors, ids, items, goals, blur_matrix(),
         params, first_moment, second_moment,
     )
     return (new_params, losses.reshape(1, 1, TILES))

time: 96.1 us -> 91.7 us (0.954)
  local copies, waits for them, and re-layouts: 6.43 us -> 2.19 us
    unnamed x20 -> x4, local copies, waits for them, and re-layouts: 6.43 us -> 2.19 us
where the time goes in v4:
time: 91.7 us; the launch traced here: 91.6 us
  Pallas kernels  88.8 us (97%)
  local copies, waits for them, and re-layouts  2.19 us (2%)
    pallas_call x1, Pallas kernels, shards(): pl.pallas_call(step, out_shape=[jax.ShapeDtypeStruct((COMP, NBLOCK * BLOC...  88.8 us
    unnamed x4, local copies, waits for them, and re-layouts  2.19 us

profile of v4, /device:TPU:1, one launch (start us, length us, event | category | flops | bytes accessed | tf_op | source)
XLA Modules:
  0.0 91.6 jit_solution(5485773465549682946)
XLA Ops:
  0.6 88.8 %shard_map.104 = (f32[7,8192]{1,0:T(8,128)}, f32[1,8]{1,0:T(1,128)}) custom-call(f32[1,4]{1,0:T(1,128)} %bitcast.20, f32[4,64]{1,0:T(4,128)} %bitcast.17, s32[2,64]{1,0:T(2,128)} %bitcast.19, s32[4,8]{1,0:T(4,128)} %bitcast.18, f32[3,8,256]{2,1,0:T(8,128)} %bitcast.16, f32[256,256]{1,0:T(8,128)} %constant.2.clone.blur_hbm, f32[7,8192]{1,0:T(8,128)} %params_hbm.1, ...), custom_call_target="tpu_custom_call" | custom-call | tf_op jit(solution)/shard_map/pallas_call | solution.py:489
  89.4 0.0 copy-start
  89.4 1.7 %copy.13 = f32[7,8192]{1,0:T(8,128)} copy(f32[7,8192]{1,0:T(8,128)} %get-tuple-element.8) | data formatting | bytes 458752
  91.1 0.0 copy-done
  91.1 0.5 copy.14
Async XLA Ops:
  89.4 1.7 %copy-start = (f32[1,8]{1,0:T(1,128)S(1)}, f32[1,8]{1,0:T(1,128)}, u32[]{:S(2)}) copy-start(f32[1,8]{1,0:T(1,128)} %get-tuple-element.5) | copy-start | bytes 100

commit v5 on v4

--- a/solution.py
+++ b/solution.py
@@ -10,6 +10,9 @@
 PIX = 256
 BLOCK = 128
 COMP = 7
+GEO = 4
+TINT = 3
+EARLY = 42
 TAPS = 11
 DEPTH = 4
 TILES = 8
@@ -83,15 +86,21 @@
 
 
 def tinted(tile):
-    level = level_of((GROUP, BLOCK))
-    shifted = jnp.concatenate([tile[4:7], tile[0:5]], axis=0)
-    return jnp.where(level == 3, 1.0, jnp.where(level < 3, shifted, 0.0))
-
-
-def derive(params_ref, camera_ref, derived):
+    filler = jnp.where(level_of((GROUP - TINT, BLOCK)) == 0, 1.0, 0.0)
+    return jnp.concatenate([tile, filler], axis=0)
+
+
+def item_rows(ref, e, count):
+    both = ref[lax.div(e, CAP)]
+    second = jnp.full((count, BLOCK), lax.rem(e, CAP), jnp.int32)
+    return jnp.where(second == 0, both[:count], both[count:])
+
+
+def derive(params_ref, camera_ref, shapes, tints):
     q0, q1, q2, q3 = (camera_ref[0, i] for i in range(4))
     width = 1024
-    derived[0] = jnp.zeros((COMP, BLOCK), F32)
+    shapes[0] = jnp.zeros((GEO, BLOCK), F32)
+    tints[0] = jnp.zeros((TINT, BLOCK), F32)
     for part in range(NBLOCK * BLOCK // width):
         values = params_ref[:, pl.ds(part * width, width)]
         row = level_of(values.shape)
@@ -105,13 +114,14 @@
         out = jnp.where(row == 1, base_w, out)
         out = jnp.where(row == 0, base_u, out)
         for i in range(width // BLOCK):
-            derived[1 + part * (width // BLOCK) + i] = out[:, i * BLOCK : (i + 1) * BLOCK]
-
-
-def forward(items_ref, rx, alphas, merged):
+            block = 1 + part * (width // BLOCK) + i
+            shapes[block] = out[:GEO, i * BLOCK : (i + 1) * BLOCK]
+            tints[block] = out[GEO:, i * BLOCK : (i + 1) * BLOCK]
+
+
+def cover(items_ref, shapes_rx, alphas, firsts, seconds, merged):
     lane = lane_of((GROUP, 128))
     level = level_of((GROUP, 128))
-    level_wide = level_of((GROUP, PIX))
     grid_x = ((lane & (SIDE - 1)).astype(F32) + 0.5) / SIDE
     grid_y = [((lane >> 4).astype(F32) + (0.5 + half * 8)) / SIDE for half in range(2)]
     halves = [pl.ds(0, 128), pl.ds(128, 128)]
@@ -119,14 +129,16 @@
     @pl.loop(0, TILES)
     def _(t):
         for k in range(DEPTH):
-            tile = rx[items_ref[k, t]]
-            cols = jnp.transpose(jnp.concatenate([tile, jnp.zeros((1, BLOCK), F32)], axis=0))
+            tile = item_rows(shapes_rx, items_ref[k, t], GEO)
+            cols = jnp.transpose(
+                jnp.concatenate([tile, jnp.zeros((GROUP - GEO, BLOCK), F32)], axis=0)
+            )
             slot = t * DEPTH + k
             clear = [jnp.ones((GROUP, 128), F32) for _ in range(2)]
             for g in range(BLOCK // GROUP):
                 rows = slice(g * GROUP, (g + 1) * GROUP)
                 u, w, inverse, opacity = (
-                    jnp.broadcast_to(cols[rows, i : i + 1], (GROUP, 128)) for i in range(4)
+                    jnp.broadcast_to(cols[rows, i : i + 1], (GROUP, 128)) for i in range(GEO)
                 )
                 dx = grid_x - u
                 dx2 = dx * dx
@@ -137,11 +149,8 @@
                     clear[half] = clear[half] * (1.0 - alpha)
             alpha = alphas[slot]
             first = alpha.astype(BF16)
-            second = (alpha - first.astype(F32)).astype(BF16)
-            wh, wm, _ = split(tinted(tile))
-            both = product(stack([wh, wm]), first)
-            rest = product(stack([wh, wh]), second)
-            sums = both[0:8] + both[8:16] + rest[0:8]
+            firsts[slot] = first
+            seconds[slot] = (alpha - first.astype(F32)).astype(BF16)
             for half in range(2):
                 p = clear[half]
                 for step in (4, 2, 1):
@@ -149,6 +158,19 @@
                 merged[0, k, :, halves[half]] = jnp.where(
                     level == t, p, merged[0, k, :, halves[half]]
                 )
+
+
+def colour(items_ref, tints_rx, firsts, seconds, merged):
+    level_wide = level_of((GROUP, PIX))
+
+    @pl.loop(0, TILES)
+    def _(t):
+        for k in range(DEPTH):
+            slot = t * DEPTH + k
+            wh, wm, _ = split(tinted(item_rows(tints_rx, items_ref[k, t], TINT)))
+            both = product(stack([wh, wm]), firsts[slot])
+            rest = product(stack([wh, wh]), seconds[slot])
+            sums = both[0:8] + both[8:16] + rest[0:8]
             for i, at in enumerate((3, 0, 1, 2)):
                 merged[1 + i, k] = jnp.where(
                     level_wide == t, sums[at : at + 1], merged[1 + i, k]
@@ -188,7 +210,7 @@
     count = 3.0 * PIX
     loss = jnp.sum(per_tile, axis=1, keepdims=True) / count
     square = (TILES, TILES)
-    loss_ref[...] = jnp.sum(
+    loss_ref[0] = jnp.sum(
         jnp.where(level_of(square) == lane_of(square), loss, 0.0), axis=0, keepdims=True
     )
 
@@ -228,7 +250,24 @@
         g_front = sum(g_ch[ch] * colours[k][ch] for ch in range(3)) + transmit * g_front
 
 
-def backward(camera_ref, items_ref, rx, alphas, back, item_grads):
+def backward_tints(items_ref, tints_rx, firsts, seconds, back, item_tints):
+    along = ((1,), (1,))
+
+    @pl.loop(0, TILES)
+    def _(t):
+        for k in range(DEPTH):
+            tone = item_rows(tints_rx, items_ref[k, t], TINT)
+            slot = t * DEPTH + k
+            rh, rm, _ = split(back[t, k])
+            both = product(stack([rh, rm]), firsts[slot], along)
+            rest = product(stack([rh, rh]), seconds[slot], along)
+            sums = both[0:TINT] + both[8 : 8 + TINT] + rest[0:TINT]
+            item_tints[slot] = jnp.concatenate(
+                [tone * (1.0 - tone) * sums, jnp.zeros((1, BLOCK), F32)], axis=0
+            )
+
+
+def backward_shapes(camera_ref, items_ref, shapes_rx, tints_rx, alphas, back, item_shapes):
     q0, q1, q2, q3 = (camera_ref[0, i] for i in range(4))
     place = lane_of((16, PIX))
     kind = level_of((16, PIX))
@@ -242,47 +281,55 @@
     @pl.loop(0, TILES)
     def _(t):
         for k in range(DEPTH):
-            tile = rx[items_ref[k, t]]
+            e = items_ref[k, t]
+            tile = item_rows(shapes_rx, e, GEO)
             slot = t * DEPTH + k
             rays = back[t, k]
             alpha = alphas[slot]
-            ah, am, al = split(tinted(tile))
+            ah, am, al = split(tinted(item_rows(tints_rx, e, TINT)))
             rh, rm, rl = split(rays)
             slope = product(
                 stack([ah, ah, am, am, ah, al]), stack([rh, rm, rh, rm, rl, rh]), ((0,), (0,))
             )
             q = (slope - rays[4:5] / (1.0 - alpha)) * alpha
             moments = sum(product(basis, part, along) for part in split(q))
-            first = alpha.astype(BF16)
-            second = (alpha - first.astype(F32)).astype(BF16)
-            both = product(stack([rh, rm]), first, along)
-            tints = both[0:3] + both[8:11] + product(stack([rh, rh]), second, along)[0:3]
             m0, mx, my, mr = (moments[i : i + 1] for i in range(4))
             cu, cw = tile[0:1] - 0.5, tile[1:2] - 0.5
             twice = 2.0 * tile[2:3]
             du = twice * (mx - cu * m0)
             dw = twice * (my - cw * m0)
             spread = mr - 2.0 * (cu * mx + cw * my) + (cu * cu + cw * cw) * m0
-            tone = tile[4:7]
-            item_grads[slot] = jnp.concatenate(
+            item_shapes[slot] = jnp.concatenate(
                 [
                     (1.0 + q0) * du + q2 * dw,
                     q1 * du + (1.0 + q3) * dw,
                     twice * spread,
                     (1.0 - tile[3:4] / OPACITY_CAP) * m0,
-                    tone * (1.0 - tone) * tints,
-                    jnp.zeros((1, BLOCK), F32),
                 ],
                 axis=0,
             )
 
 
+def to_slots(items, place, out, count):
+    parts = split(jnp.concatenate([items[i] for i in range(TILES * DEPTH)], axis=0))
+    chunk = 256
+    for part in range(NCELL * CAP * GEO // chunk):
+        at = (level_of((chunk, TILES * DEPTH * GEO)) + part * chunk).astype(F32)
+        spots = jnp.where(at == place, 1.0, 0.0).astype(BF16)
+        found = sum(product(spots, x) for x in parts)
+        for i in range(chunk // (CAP * GEO)):
+            first, second = (found[(CAP * i + j) * GEO :][:count] for j in range(CAP))
+            out[part * (chunk // (CAP * GEO)) + i] = jnp.concatenate([first, second], axis=0)
+
+
 def step(
     camera_hbm, anchor_hbm, ids_hbm, items_hbm, goal_hbm, blur_hbm,
     params_hbm, first_hbm, second_hbm, out_ref, loss_ref,
-    camera_ref, ids_ref, anchor_ref, items_ref, params_ref, first_ref, second_ref, ids_rows, items_rows, goal_ref, blur_ref, derived, tx, rx, alphas, merged, back, item_grads,
-    grads, grads_rx, summed, shares, rows, mine,
-    stage_sem, send_sem, recv_sem, back_send, back_recv, part_send, part_recv, row_send, row_recv,
+    camera_ref, ids_ref, anchor_ref, items_ref, params_ref, first_ref, second_ref, ids_rows, items_rows, goal_ref, blur_ref,
+    shapes, tints, shapes_tx, tints_tx, shapes_rx, tints_rx, alphas, firsts, seconds, merged, back,
+    item_shapes, item_tints, shapes_back, tints_back, shapes_home, tints_home, summed, shares, rows, mine,
+    stage_sem, early_send, late_send, shape_recv, tint_send, tint_recv,
+    home_tint_send, home_tint_recv, home_send, home_recv, part_send, part_recv, row_send, row_recv,
 ):
     c = lax.axis_index("cell")
     v = lax.axis_index("view")
@@ -323,35 +370,39 @@
 
     for i in (0, 7, 8, 9, 10):
         staged[i].wait()
-    derive(params_ref, camera_ref, derived)
+    derive(params_ref, camera_ref, shapes, tints)
     pl.semaphore_wait(barrier, NCELL - 1 + NVIEW - 1)
 
-    def pair(o):
-        return pl.ds(o * CAP, CAP)
-
     def gather(o):
-        row = level_of((COMP, BLOCK))
-        for j in range(CAP):
-            shift = jnp.where(
-                row == 0, anchor_ref[j, o], jnp.where(row == 1, anchor_ref[CAP + j, o], 0.0)
-            )
-            tx[o * CAP + j] = derived[ids_ref[j, o] + 1] + shift
-
-    @pl.loop(0, NCELL - 1, unroll=3)
-    def _(i):
-        o = cell_peer(i, z, y)
-        gather(o)
+        row = level_of((GEO, BLOCK))
+        blocks = [ids_ref[j, o] + 1 for j in range(CAP)]
+        shifts = [
+            jnp.where(row == 0, anchor_ref[j, o], jnp.where(row == 1, anchor_ref[CAP + j, o], 0.0))
+            for j in range(CAP)
+        ]
+        shapes_tx[o] = jnp.concatenate([shapes[b] + s for b, s in zip(blocks, shifts)], axis=0)
+        tints_tx[o] = jnp.concatenate([tints[b] for b in blocks], axis=0)
+
+    def send(source, target, o, send_sem, recv_sem):
         pltpu.make_async_remote_copy(
-            src_ref=tx.at[pair(o)],
-            dst_ref=rx.at[pair(c)],
+            src_ref=source,
+            dst_ref=target,
             send_sem=send_sem,
             recv_sem=recv_sem,
             device_id=(o, v),
             device_id_type=MESH,
         ).start()
 
+    for low, high, sem in ((0, EARLY, early_send), (EARLY, NCELL - 1, late_send)):
+
+        @pl.loop(low, high, unroll=3)
+        def _(i):
+            o = cell_peer(i, z, y)
+            gather(o)
+            send(shapes_tx.at[o], shapes_rx.at[c], o, sem, shape_recv)
+
     gather(c)
-    pltpu.make_async_copy(tx.at[pair(c)], rx.at[pair(c)], recv_sem).start()
+    pltpu.make_async_copy(shapes_tx.at[c], shapes_rx.at[c], shape_recv).start()
 
     for copy in staged[1:7]:
         copy.wait()
@@ -367,47 +418,49 @@
             mine[i, pl.ds(b, 1), :] = jnp.sum(only, axis=0, keepdims=True)
     back[...] = jnp.zeros((TILES, DEPTH, GROUP, PIX), F32)
     merged[...] = jnp.zeros((5, DEPTH, TILES, PIX), F32)
-    wide = (TILES, TILES * DEPTH * GROUP)
-    place = lax.rem(lane_of((1, wide[1])), GROUP).astype(F32)
+    wide = (TILES, TILES * DEPTH * GEO)
+    place = lax.rem(lane_of((1, wide[1])), GEO).astype(F32)
     for k in range(DEPTH):
-        pick = jnp.where(lax.div(lane_of(wide), GROUP) == level_of(wide) * DEPTH + k, 1.0, 0.0)
+        pick = jnp.where(lax.div(lane_of(wide), GEO) == level_of(wide) * DEPTH + k, 1.0, 0.0)
         entries = jnp.broadcast_to(items_rows[k : k + 1, :].astype(F32), (TILES, TILES))
-        place = place + GROUP * product(entries.astype(BF16), pick.astype(BF16))[0:1]
-
-    pltpu.make_async_copy(tx, rx, recv_sem).wait()
-
-    forward(items_ref, rx, alphas, merged)
-    compare(merged, goals, goal_blur, blur_ref, loss_ref, back)
-    backward(camera_ref, items_ref, rx, alphas, back, item_grads)
-
-    parts = split(item_grads[...].reshape(TILES * DEPTH * GROUP, BLOCK))
-    chunk = 256
-    for part in range(NCELL * CAP * GROUP // chunk):
-        at = (level_of((chunk, wide[1])) + part * chunk).astype(F32)
-        spots = jnp.where(at == place, 1.0, 0.0).astype(BF16)
-        found = sum(product(spots, x) for x in parts)
-        for i in range(chunk // GROUP):
-            slot = part * (chunk // GROUP) + i
-            grads[slot // CAP, slot % CAP] = found[i * GROUP : i * GROUP + COMP]
+        place = place + GEO * product(entries.astype(BF16), pick.astype(BF16))[0:1]
+
+    def done(source, target, first, count, sem):
+        span = pl.ds(first, count)
+        pltpu.make_async_copy(source.at[span], target.at[span], sem).wait()
+
+    done(shapes_tx, shapes_rx, 0, EARLY, early_send)
 
     @pl.loop(0, NCELL - 1, unroll=9)
     def _(i):
         o = cell_peer(i, z, y)
-        pltpu.make_async_remote_copy(
-            src_ref=grads.at[o],
-            dst_ref=grads_rx.at[c],
-            send_sem=back_send,
-            recv_sem=back_recv,
-            device_id=(o, v),
-            device_id_type=MESH,
-        ).start()
-
-    pltpu.make_async_copy(grads.at[c], grads_rx.at[c], back_recv).start()
-    pltpu.make_async_copy(grads, grads_rx, back_recv).wait()
-
-    for p in range(COMP):
-        values = jnp.concatenate([grads_rx[:, j, p, :] for j in range(CAP)], axis=0)
-        summed[p] = jnp.dot(chosen, values, precision=HIGHEST, preferred_element_type=F32)
+        send(tints_tx.at[o], tints_rx.at[c], o, tint_send, tint_recv)
+
+    pltpu.make_async_copy(tints_tx.at[c], tints_rx.at[c], tint_recv).start()
+
+    pltpu.make_async_copy(shapes_tx, shapes_rx, shape_recv).wait()
+    cover(items_ref, shapes_rx, alphas, firsts, seconds, merged)
+    pltpu.make_async_copy(tints_tx, tints_rx, tint_recv).wait()
+    colour(items_ref, tints_rx, firsts, seconds, merged)
+    compare(merged, goals, goal_blur, blur_ref, loss_ref, back)
+    backward_tints(items_ref, tints_rx, firsts, seconds, back, item_tints)
+    to_slots(item_tints, place, tints_back, TINT)
+
+    @pl.loop(0, NCELL - 1, unroll=9)
+    def _(i):
+        o = cell_peer(i, z, y)
+        send(tints_back.at[o], tints_home.at[c], o, home_tint_send, home_tint_recv)
+
+    pltpu.make_async_copy(tints_back.at[c], tints_home.at[c], home_tint_recv).start()
+    backward_shapes(camera_ref, items_ref, shapes_rx, tints_rx, alphas, back, item_shapes)
+    to_slots(item_shapes, place, shapes_back, GEO)
+
+    @pl.loop(0, NCELL - 1, unroll=9)
+    def _(i):
+        o = cell_peer(i, z, y)
+        send(shapes_back.at[o], shapes_home.at[c], o, home_send, home_recv)
+
+    pltpu.make_async_copy(shapes_back.at[c], shapes_home.at[c], home_recv).start()
 
     def part(i):
         w = lax.rem(v + i, NVIEW)
@@ -423,9 +476,19 @@
     def arrived(buffer, sem, s):
         return pltpu.make_async_copy(buffer.at[s], buffer.at[s], sem.at[s])
 
-    for i in range(1, NVIEW):
-        w, copy = part(i)
-        pl.when(w < COMP)(copy.start)
+    for source, target, sem, low, high in (
+        (tints_back, tints_home, home_tint_recv, GEO, COMP),
+        (shapes_back, shapes_home, home_recv, 0, GEO),
+    ):
+        pltpu.make_async_copy(source, target, sem).wait()
+        for p in range(low, high):
+            values = jnp.concatenate(
+                [target[:, j * (high - low) + p - low, :] for j in range(CAP)], axis=0
+            )
+            summed[p] = jnp.dot(chosen, values, precision=HIGHEST, preferred_element_type=F32)
+        for i in range(1, NVIEW):
+            w, copy = part(i)
+            pl.when((w >= low) & (w < high))(copy.start)
 
     def send_row(i):
         return pltpu.make_async_remote_copy(
@@ -458,10 +521,10 @@
         for b in range(NBLOCK):
             out_ref[pl.ds(p, 1), pl.ds(b * BLOCK, BLOCK)] = rows[p, pl.ds(b, 1), :]
 
-    rest = pl.ds(0, CAP * (NCELL - 1))
-    pltpu.make_async_copy(tx.at[rest], rx.at[rest], send_sem).wait()
-    rest = pl.ds(0, NCELL - 1)
-    pltpu.make_async_copy(grads.at[rest], grads_rx.at[rest], back_send).wait()
+    done(shapes_tx, shapes_rx, 0, NCELL - 1 - EARLY, late_send)
+    done(tints_tx, tints_rx, 0, NCELL - 1, tint_send)
+    done(tints_back, tints_home, 0, NCELL - 1, home_tint_send)
+    done(shapes_back, shapes_home, 0, NCELL - 1, home_send)
     for i in range(1, NVIEW):
         w, copy = part(i)
         pl.when(w < COMP)(copy.wait_send)
@@ -481,8 +544,6 @@
     anchors = jnp.transpose(slot_anchor[0, 0, 0], (0, 2, 1)).reshape(2 * CAP, NCELL)
     items = jnp.transpose(tile_items[0, 0], (1, 0))
     goals = jnp.transpose(target[0, 0], (1, 0, 2))
-    message = pltpu.VMEM((NCELL * CAP, COMP, BLOCK), F32)
-    returned = pltpu.VMEM((NCELL, CAP, COMP, BLOCK), F32)
     whole = pltpu.VMEM((COMP, NBLOCK * BLOCK), F32)
     table = pltpu.VMEM((COMP, NBLOCK, BLOCK), F32)
     dma = pltpu.SemaphoreType.DMA
@@ -490,7 +551,7 @@
         step,
         out_shape=[
             jax.ShapeDtypeStruct((COMP, NBLOCK * BLOCK), F32),
-            jax.ShapeDtypeStruct((1, TILES), F32),
+            jax.ShapeDtypeStruct((1, 1, TILES), F32),
         ],
         in_specs=[hbm] * 9,
         out_specs=[vmem, vmem],
@@ -506,24 +567,29 @@
             pltpu.VMEM((DEPTH, TILES), jnp.int32),
             pltpu.VMEM((3, TILES, PIX), F32),
             pltpu.VMEM((PIX, PIX), F32),
-            pltpu.VMEM((1 + NBLOCK, COMP, BLOCK), F32),
-            message,
-            message,
+            pltpu.VMEM((1 + NBLOCK, GEO, BLOCK), F32),
+            pltpu.VMEM((1 + NBLOCK, TINT, BLOCK), F32),
+            pltpu.VMEM((NCELL, CAP * GEO, BLOCK), F32),
+            pltpu.VMEM((NCELL, CAP * TINT, BLOCK), F32),
+            pltpu.VMEM((NCELL, CAP * GEO, BLOCK), F32),
+            pltpu.VMEM((NCELL, CAP * TINT, BLOCK), F32),
             pltpu.VMEM((TILES * DEPTH, BLOCK, PIX), F32),
+            pltpu.VMEM((TILES * DEPTH, BLOCK, PIX), BF16),
+            pltpu.VMEM((TILES * DEPTH, BLOCK, PIX), BF16),
             pltpu.VMEM((5, DEPTH, TILES, PIX), F32),
             pltpu.VMEM((TILES, DEPTH, GROUP, PIX), F32),
-            pltpu.VMEM((TILES * DEPTH, GROUP, BLOCK), F32),
-            returned,
-            returned,
+            pltpu.VMEM((TILES * DEPTH, GEO, BLOCK), F32),
+            pltpu.VMEM((TILES * DEPTH, GEO, BLOCK), F32),
+            pltpu.VMEM((NCELL, CAP * GEO, BLOCK), F32),
+            pltpu.VMEM((NCELL, CAP * TINT, BLOCK), F32),
+            pltpu.VMEM((NCELL, CAP * GEO, BLOCK), F32),
+            pltpu.VMEM((NCELL, CAP * TINT, BLOCK), F32),
             table,
             pltpu.VMEM((NVIEW, NBLOCK, BLOCK), F32),
             table,
             pltpu.VMEM((3, NBLOCK, BLOCK), F32),
             dma((11,)),
-            dma,
-            dma,
-            dma,
-            dma,
+            *[dma] * 9,
             dma((NVIEW,)),
             dma((NVIEW,)),
             dma((NVIEW,)),
@@ -536,7 +602,7 @@
         camera[0], anchors, ids, items, goals, blur_matrix(),
         params, first_moment, second_moment,
     )
-    return (new_params, losses.reshape(1, 1, TILES))
+    return (new_params, losses)
 
 
 def solution(mesh):

time: 91.7 us -> 82.1 us (0.90)
  Pallas kernels: 88.8 us -> 79.1 us
    pallas_call x1, Pallas kernels: 88.8 us -> 79.1 us  [shards(): pl.pallas_call(step, out_shape=[jax.ShapeDtypeStruct((COMP, NBLOCK * BLOC...]
where the time goes in v5:
time: 82.1 us; the launch traced here: 81.9 us
  Pallas kernels  79.1 us (96%)
  local copies, waits for them, and re-layouts  2.19 us (3%)
    pallas_call x1, Pallas kernels, shards(): pl.pallas_call(step, out_shape=[jax.ShapeDtypeStruct((COMP, NBLOCK * BLOC...  79.1 us
    unnamed x4, local copies, waits for them, and re-layouts  2.19 us

profile of v5, /device:TPU:1, one launch (start us, length us, event | category | flops | bytes accessed | tf_op | source)
XLA Modules:
  0.0 81.9 jit_solution(9418910655199842784)
XLA Ops:
  0.6 79.1 %shard_map.104 = (f32[7,8192]{1,0:T(8,128)}, f32[1,1,8]{2,1,0:T(1,128)}) custom-call(f32[1,4]{1,0:T(1,128)} %bitcast.19, f32[4,64]{1,0:T(4,128)} %bitcast.16, s32[2,64]{1,0:T(2,128)} %bitcast.18, s32[4,8]{1,0:T(4,128)} %bitcast.17, f32[3,8,256]{2,1,0:T(8,128)} %bitcast.15, f32[256,256]{1,0:T(8,128)} %constant.2.clone.blur_hbm, f32[7,8192]{1,0:T(8,128)} %params_hbm.1, ...), custom_call_target="tpu_custom_call" | custom-call | tf_op jit(solution)/shard_map/pallas_call | solution.py:550
  79.7 0.0 copy-start
  79.8 1.7 %copy.13 = f32[7,8192]{1,0:T(8,128)} copy(f32[7,8192]{1,0:T(8,128)} %get-tuple-element.4) | data formatting | bytes 458752
  81.4 0.0 copy-done
  81.4 0.5 copy.14
Async XLA Ops:
  79.7 1.7 %copy-start = (f32[1,1,8]{2,1,0:T(1,128)S(1)}, f32[1,1,8]{2,1,0:T(1,128)}, u32[]{:S(2)}) copy-start(f32[1,1,8]{2,1,0:T(1,128)} %get-tuple-element.5) | copy-start | bytes 100

commit v6 on v5

--- a/solution.py
+++ b/solution.py
@@ -13,6 +13,7 @@
 GEO = 4
 TINT = 3
 EARLY = 42
+FAR_FIRST = (4, 3, 5, 2, 6, 7, 1)
 TAPS = 11
 DEPTH = 4
 TILES = 8
@@ -54,6 +55,10 @@
     m = lax.div(k + 1, 2)
     dz = jnp.where(lax.rem(k, 2) == 1, m, NZ - m)
     return lax.rem(z + dz, NZ) * NY + lax.rem(y + lax.rem(i, NY), NY)
+
+
+def row_of(v):
+    return lax.div(v, 2) + GEO * lax.rem(v, 2)
 
 
 def split(x):
@@ -373,15 +378,18 @@
     derive(params_ref, camera_ref, shapes, tints)
     pl.semaphore_wait(barrier, NCELL - 1 + NVIEW - 1)
 
-    def gather(o):
+    def gather_shapes(o):
         row = level_of((GEO, BLOCK))
-        blocks = [ids_ref[j, o] + 1 for j in range(CAP)]
         shifts = [
             jnp.where(row == 0, anchor_ref[j, o], jnp.where(row == 1, anchor_ref[CAP + j, o], 0.0))
             for j in range(CAP)
         ]
-        shapes_tx[o] = jnp.concatenate([shapes[b] + s for b, s in zip(blocks, shifts)], axis=0)
-        tints_tx[o] = jnp.concatenate([tints[b] for b in blocks], axis=0)
+        shapes_tx[o] = jnp.concatenate(
+            [shapes[ids_ref[j, o] + 1] + shifts[j] for j in range(CAP)], axis=0
+        )
+
+    def gather_tints(o):
+        tints_tx[o] = jnp.concatenate([tints[ids_ref[j, o] + 1] for j in range(CAP)], axis=0)
 
     def send(source, target, o, send_sem, recv_sem):
         pltpu.make_async_remote_copy(
@@ -398,10 +406,10 @@
         @pl.loop(low, high, unroll=3)
         def _(i):
             o = cell_peer(i, z, y)
-            gather(o)
+            gather_shapes(o)
             send(shapes_tx.at[o], shapes_rx.at[c], o, sem, shape_recv)
 
-    gather(c)
+    gather_shapes(c)
     pltpu.make_async_copy(shapes_tx.at[c], shapes_rx.at[c], shape_recv).start()
 
     for copy in staged[1:7]:
@@ -410,7 +418,8 @@
     goal_blur = blurred(jnp.concatenate([goals, goals * goals], axis=0), blur_ref[...])
     ids = jnp.concatenate([ids_rows[0:1, :], ids_rows[1:2, :]], axis=1)
     chosen = jnp.where(level_of((NBLOCK, CAP * NCELL)) == ids, 1.0, 0.0).astype(F32)
-    row = jnp.minimum(v, COMP - 1)
+    own = row_of(v)
+    row = jnp.minimum(own, COMP - 1)
     level = level_of((COMP, BLOCK))
     for b in range(NBLOCK):
         for i, ref in enumerate((params_ref, first_ref, second_ref)):
@@ -431,11 +440,13 @@
 
     done(shapes_tx, shapes_rx, 0, EARLY, early_send)
 
-    @pl.loop(0, NCELL - 1, unroll=9)
+    @pl.loop(0, NCELL - 1, unroll=3)
     def _(i):
         o = cell_peer(i, z, y)
+        gather_tints(o)
         send(tints_tx.at[o], tints_rx.at[c], o, tint_send, tint_recv)
 
+    gather_tints(c)
     pltpu.make_async_copy(tints_tx.at[c], tints_rx.at[c], tint_recv).start()
 
     pltpu.make_async_copy(shapes_tx, shapes_rx, shape_recv).wait()
@@ -465,7 +476,7 @@
     def part(i):
         w = lax.rem(v + i, NVIEW)
         return w, pltpu.make_async_remote_copy(
-            src_ref=summed.at[jnp.minimum(w, COMP - 1)],
+            src_ref=summed.at[jnp.minimum(row_of(w), COMP - 1)],
             dst_ref=shares.at[v],
             send_sem=part_send.at[i],
             recv_sem=part_recv.at[v],
@@ -486,9 +497,9 @@
                 [target[:, j * (high - low) + p - low, :] for j in range(CAP)], axis=0
             )
             summed[p] = jnp.dot(chosen, values, precision=HIGHEST, preferred_element_type=F32)
-        for i in range(1, NVIEW):
+        for i in FAR_FIRST:
             w, copy = part(i)
-            pl.when((w >= low) & (w < high))(copy.start)
+            pl.when((row_of(w) >= low) & (row_of(w) < high))(copy.start)
 
     def send_row(i):
         return pltpu.make_async_remote_copy(
@@ -513,11 +524,11 @@
         fix_one = 1.0 - BETA_ONE**FIRST_STEP
         fix_two = 1.0 - BETA_TWO**FIRST_STEP
         rows[row] = mine[0] - LEARN_RATE * (one / fix_one) / (jnp.sqrt(two / fix_two) + ADAM_EPS)
-        for i in range(1, NVIEW):
+        for i in FAR_FIRST:
             send_row(i).start()
 
-    for p in range(COMP):
-        pl.when(v != p)(arrived(rows, row_recv, p).wait)
+    for p in (*range(GEO, COMP), *range(GEO)):
+        pl.when(own != p)(arrived(rows, row_recv, p).wait)
         for b in range(NBLOCK):
             out_ref[pl.ds(p, 1), pl.ds(b * BLOCK, BLOCK)] = rows[p, pl.ds(b, 1), :]
 

time: 82.1 us -> 81.1 us (0.988)
  Pallas kernels: 79.1 us -> 78.1 us
    pallas_call x1, Pallas kernels: 79.1 us -> 78.1 us  [shards(): pl.pallas_call(step, out_shape=[jax.ShapeDtypeStruct((COMP, NBLOCK * BLOC...]
where the time goes in v6:
time: 81.1 us; the launch traced here: 81 us
  Pallas kernels  78.1 us (96%)
  local copies, waits for them, and re-layouts  2.19 us (3%)
    pallas_call x1, Pallas kernels, shards(): pl.pallas_call(step, out_shape=[jax.ShapeDtypeStruct((COMP, NBLOCK * BLOC...  78.1 us
    unnamed x4, local copies, waits for them, and re-layouts  2.19 us

profile of v6, /device:TPU:1, one launch (start us, length us, event | category | flops | bytes accessed | tf_op | source)
XLA Modules:
  0.0 81.0 jit_solution(329819156371842727)
XLA Ops:
  0.6 78.1 %shard_map.104 = (f32[7,8192]{1,0:T(8,128)}, f32[1,1,8]{2,1,0:T(1,128)}) custom-call(f32[1,4]{1,0:T(1,128)} %bitcast.19, f32[4,64]{1,0:T(4,128)} %bitcast.16, s32[2,64]{1,0:T(2,128)} %bitcast.18, s32[4,8]{1,0:T(4,128)} %bitcast.17, f32[3,8,256]{2,1,0:T(8,128)} %bitcast.15, f32[256,256]{1,0:T(8,128)} %constant.2.clone.blur_hbm, f32[7,8192]{1,0:T(8,128)} %params_hbm.1, ...), custom_call_target="tpu_custom_call" | custom-call | tf_op jit(solution)/shard_map/pallas_call | solution.py:561
  78.8 0.0 copy-start
  78.8 1.7 %copy.13 = f32[7,8192]{1,0:T(8,128)} copy(f32[7,8192]{1,0:T(8,128)} %get-tuple-element.4) | data formatting | bytes 458752
  80.4 0.0 copy-done
  80.4 0.5 copy.14
Async XLA Ops:
  78.8 1.7 %copy-start = (f32[1,1,8]{2,1,0:T(1,128)S(1)}, f32[1,1,8]{2,1,0:T(1,128)}, u32[]{:S(2)}) copy-start(f32[1,1,8]{2,1,0:T(1,128)} %get-tuple-element.5) | copy-start | bytes 100

commit v7 on v6

--- a/solution.py
+++ b/solution.py
@@ -417,7 +417,7 @@
     goals = jnp.concatenate([goal_ref[ch] for ch in range(3)], axis=0)
     goal_blur = blurred(jnp.concatenate([goals, goals * goals], axis=0), blur_ref[...])
     ids = jnp.concatenate([ids_rows[0:1, :], ids_rows[1:2, :]], axis=1)
-    chosen = jnp.where(level_of((NBLOCK, CAP * NCELL)) == ids, 1.0, 0.0).astype(F32)
+    chosen = jnp.where(level_of((NBLOCK, CAP * NCELL)) == ids, 1.0, 0.0).astype(BF16)
     own = row_of(v)
     row = jnp.minimum(own, COMP - 1)
     level = level_of((COMP, BLOCK))
@@ -496,7 +496,7 @@
             values = jnp.concatenate(
                 [target[:, j * (high - low) + p - low, :] for j in range(CAP)], axis=0
             )
-            summed[p] = jnp.dot(chosen, values, precision=HIGHEST, preferred_element_type=F32)
+            summed[p] = sum(product(chosen, x) for x in split(values))
         for i in FAR_FIRST:
             w, copy = part(i)
             pl.when((row_of(w) >= low) & (row_of(w) < high))(copy.start)

time: 81.1 us -> 81 us (level)
  no operation moved by 1% of the time
where the time goes in v7:
time: 81 us; the launch traced here: 80.9 us
  Pallas kernels  78.1 us (96%)
  local copies, waits for them, and re-layouts  2.19 us (3%)
    pallas_call x1, Pallas kernels, shards(): pl.pallas_call(step, out_shape=[jax.ShapeDtypeStruct((COMP, NBLOCK * BLOC...  78.1 us
    unnamed x4, local copies, waits for them, and re-layouts  2.19 us

profile of v7, /device:TPU:1, one launch (start us, length us, event | category | flops | bytes accessed | tf_op | source)
XLA Modules:
  0.0 80.9 jit_solution(1466684480267999200)
XLA Ops:
  0.6 78.1 %shard_map.104 = (f32[7,8192]{1,0:T(8,128)}, f32[1,1,8]{2,1,0:T(1,128)}) custom-call(f32[1,4]{1,0:T(1,128)} %bitcast.19, f32[4,64]{1,0:T(4,128)} %bitcast.16, s32[2,64]{1,0:T(2,128)} %bitcast.18, s32[4,8]{1,0:T(4,128)} %bitcast.17, f32[3,8,256]{2,1,0:T(8,128)} %bitcast.15, f32[256,256]{1,0:T(8,128)} %constant.2.clone.blur_hbm, f32[7,8192]{1,0:T(8,128)} %params_hbm.1, ...), custom_call_target="tpu_custom_call" | custom-call | tf_op jit(solution)/shard_map/pallas_call | solution.py:561
  78.7 0.0 copy-start
  78.7 1.7 %copy.13 = f32[7,8192]{1,0:T(8,128)} copy(f32[7,8192]{1,0:T(8,128)} %get-tuple-element.4) | data formatting | bytes 458752
  80.4 0.0 copy-done
  80.4 0.5 copy.14
Async XLA Ops:
  78.7 1.7 %copy-start = (f32[1,1,8]{2,1,0:T(1,128)S(1)}, f32[1,1,8]{2,1,0:T(1,128)}, u32[]{:S(2)}) copy-start(f32[1,1,8]{2,1,0:T(1,128)} %get-tuple-element.5) | copy-start | bytes 100
